TPU v7x, 128 devices: a whole 4x4x4 slice. The times are simulated.
128 devices in a mesh: slab: 16 (over x, y), cross: 8 (over z, core).
Axes of the slice: x: 4, y: 4, z: 4, core: 2. Of those that a mesh axis runs over, the one named last changes fastest.
Arguments:
- rhs: float32 [64, 64, 32, 128], P(None, 'slab', 'cross'), may hold values from -6 to 6
- classes: int32 [64, 32, 128], P('slab', 'cross'), may hold values from 0 to 15
- perm: float32 [16], replicated, may hold values from 0.1 to 10
- vol_block: float32 [64, 64], replicated, may hold values from -0.72 to 3.5
- side_blocks: float32 [6, 64, 64], replicated, may hold values from -0.24 to 1.3
- couple: float32 [3, 64, 64], replicated, may hold values from -0.24 to 0.5
- smoother_blocks: float32 [16, 64, 64], replicated, may hold values from -0.024 to 0.09
- restrict_map: float32 [8, 64], replicated, may hold values from -0.75 to 0.75
- coarse_block: float32 [8, 8], replicated, may hold values from -0.048 to 0.09
- owners: int32 [16, 8, 2048, 1], P('slab', 'cross'), may hold values from 0 to 127, as said below
- agg_local: int32 [16, 8, 2048], P('slab', 'cross'), may hold values from 0 to 127
Outputs:
- solution: float32 [64, 64, 32, 128], P(None, 'slab', 'cross')
- residual: float32 [64, 64, 32, 128], P(None, 'slab', 'cross')
Inputs may be any that keep to these rules, and one draw needn't show every extreme that they name: `owners`: no owner is named by more than 32 of one device's elements, and some owner is named by exactly 32 elements of some device.
All inputs are finite; a program needn't handle non-finite values.
Results may differ from a plain program's by a relative error of at most 0.0003.
Values sent between devices are 32-bit elements; how exact they have to be, the bound alone decides.
A program may use at most 128 MiB of HBM per device.

v0:
```python
import jax
import jax.numpy as jnp
from jax import lax
from jax.sharding import PartitionSpec as P


def with_halo(array, sides, width):
    for axis, dim in sides:
        count, length = (lax.axis_size(axis), array.shape[dim])
        up = [(i, (i + 1) % count) for i in range(count - 1)]
        down = [(j, i) for i, j in up]
        last = lax.slice_in_dim(array, length - width, length, axis=dim)
        initial = lax.slice_in_dim(array, 0, width, axis=dim)
        before = lax.ppermute(last, axis, up)
        after = lax.ppermute(initial, axis, down)
        array = jnp.concatenate([before, array, after], axis=dim)
    return array


def apply_block(matrix, field):
    return jnp.einsum("ij,jabc->iabc", matrix, field, precision=lax.Precision.HIGHEST)


def neighbours(padded):
    return [
        padded[..., :-2, 1:-1, 1:-1],
        padded[..., 2:, 1:-1, 1:-1],
        padded[..., 1:-1, :-2, 1:-1],
        padded[..., 1:-1, 2:, 1:-1],
        padded[..., 1:-1, 1:-1, :-2],
        padded[..., 1:-1, 1:-1, 2:],
    ]


def cell_perm(classes, perm):
    labels = jnp.arange(perm.shape[0], dtype=jnp.int32)[:, None, None, None]
    return jnp.sum(jnp.where(classes[None] == labels, perm[:, None, None, None], 0.0), axis=0)


def face_weights(perm_cell, padded_perm):
    result = []
    for other in neighbours(padded_perm):
        result.append(
            jnp.where(other > 0.0, 2.0 * perm_cell * other / (perm_cell + other), 2.0 * perm_cell)
        )
    return result


def operate(field, padded_field, perm_cell, weights, vol_block, side_blocks, couple):
    result = perm_cell * apply_block(vol_block, field)
    others = neighbours(padded_field)
    for direction in range(6):
        coupling = couple[direction // 2]
        if direction % 2 == 0:
            coupling = coupling.T
        result = result + weights[direction] * (
            apply_block(side_blocks[direction], field) - apply_block(coupling, others[direction])
        )
    return result


def fill_slots(values, slot_of, owner_count, slot_cap):
    buffer = (
        jnp.zeros((values.shape[0], owner_count * slot_cap), values.dtype)
        .at[:, slot_of]
        .set(values)
    )
    return buffer.reshape(values.shape[0], owner_count, slot_cap)


def local(
    rhs,
    classes,
    perm,
    vol_block,
    side_blocks,
    couple,
    smoother_blocks,
    restrict_map,
    coarse_block,
    owners,
    agg_local,
):
    node_count = rhs.shape[0]
    perm_cell = cell_perm(classes, perm)
    rim_perm = with_halo(perm_cell, (("slab", 0), ("cross", 1)), 1)
    weights = face_weights(perm_cell, jnp.pad(rim_perm, ((0, 0), (0, 0), (1, 1))))
    owner_count = lax.axis_size("slab") * lax.axis_size("cross")
    owner_flat = owners.reshape(-1)
    local_flat = agg_local.reshape(-1)
    element_count = owner_flat.shape[0]
    slot_cap = 2 * element_count // owner_count
    agg_count = 4 * slot_cap
    class_flat = classes.reshape(-1)
    class_total = smoother_blocks.shape[0]
    tile_width = min(128, max(1, element_count // class_total))
    tile_count = element_count // tile_width + class_total
    class_labels = jnp.arange(class_total, dtype=jnp.int32)
    per_class = jnp.sum((class_flat[:, None] == class_labels[None, :]).astype(jnp.int32), axis=0)
    padded_count = (per_class + tile_width - 1) // tile_width * tile_width
    padded_start = jnp.cumsum(padded_count) - padded_count
    plain_start = jnp.cumsum(per_class) - per_class
    class_order = jnp.argsort(class_flat, stable=True)
    sorted_class = class_flat[class_order]
    bucket_pos = (
        padded_start[sorted_class]
        + jnp.arange(element_count, dtype=jnp.int32)
        - plain_start[sorted_class]
    )
    tile_first = jnp.arange(tile_count, dtype=jnp.int32) * tile_width
    tile_class = jnp.clip(
        jnp.sum((padded_start[None, :] <= tile_first[:, None]).astype(jnp.int32), axis=1) - 1,
        0,
        class_total - 1,
    )
    tile_blocks = smoother_blocks[tile_class]

    def smooth(iterate, residue):
        flat = residue.reshape(node_count, -1)
        bucket = (
            jnp.zeros((node_count, tile_count * tile_width), jnp.float32)
            .at[:, bucket_pos]
            .set(flat[:, class_order])
        )
        bucket = bucket.reshape(node_count, tile_count, tile_width)
        applied = jnp.einsum(
            "tij,jtk->itk", tile_blocks, bucket, precision=lax.Precision.HIGHEST
        ).reshape(node_count, -1)
        update = (
            jnp.zeros((node_count, element_count), jnp.float32)
            .at[:, class_order]
            .set(applied[:, bucket_pos])
        )
        return iterate + update.reshape(residue.shape) / perm_cell

    def fine_op(field):
        padded = with_halo(field, (("slab", 1), ("cross", 2)), 1)
        padded = jnp.pad(padded, ((0, 0), (0, 0), (0, 0), (1, 1)))
        return operate(field, padded, perm_cell, weights, vol_block, side_blocks, couple)

    def sweep(iterate):
        return smooth(iterate, rhs - fine_op(iterate))

    def move_floats(buffer):
        return lax.all_to_all(buffer, ("slab", "cross"), split_axis=1, concat_axis=1, tiled=True)

    counts = jnp.sum(
        (owner_flat[:, None] == jnp.arange(owner_count, dtype=jnp.int32)[None, :]).astype(
            jnp.int32
        ),
        axis=0,
    )
    starts = jnp.cumsum(counts) - counts
    ordering = jnp.argsort(owner_flat, stable=True)
    sorted_owner = owner_flat[ordering]
    slot_sorted = (
        sorted_owner * slot_cap + jnp.arange(element_count, dtype=jnp.int32) - starts[sorted_owner]
    )
    slot_of = jnp.zeros((element_count,), jnp.int32).at[ordering].set(slot_sorted)
    id_buffer = jnp.zeros((owner_count * slot_cap,), jnp.int32).at[slot_of].set(local_flat)
    received_ids = lax.all_to_all(
        id_buffer.reshape(1, owner_count, slot_cap),
        ("slab", "cross"),
        split_axis=1,
        concat_axis=1,
        tiled=True,
    ).reshape(-1)

    def to_owner(values):
        arrived = move_floats(fill_slots(values, slot_of, owner_count, slot_cap)).reshape(
            values.shape[0], -1
        )
        return jax.ops.segment_sum(arrived.T, received_ids, agg_count).T

    def from_owner(coarse):
        outgoing = coarse[:, received_ids].reshape(coarse.shape[0], owner_count, slot_cap)
        return move_floats(outgoing).reshape(coarse.shape[0], -1)[:, slot_of]

    def restrict(field):
        return to_owner(
            jnp.dot(restrict_map, field.reshape(node_count, -1), precision=lax.Precision.HIGHEST)
        )

    def prolong(coarse):
        return jnp.dot(restrict_map.T, from_owner(coarse), precision=lax.Precision.HIGHEST).reshape(
            rhs.shape
        )

    perm_sum = to_owner(perm_cell.reshape(1, -1))[0]
    coarse_scale = 1.0 / (1.0 + perm_sum)
    iterate = smooth(jnp.zeros_like(rhs), rhs)
    iterate = sweep(iterate)
    fine_res = rhs - fine_op(iterate)
    coarse_res = restrict(fine_res)
    first = coarse_scale * jnp.dot(coarse_block, coarse_res, precision=lax.Precision.HIGHEST)
    again = coarse_res - restrict(fine_op(prolong(first)))
    second = first + coarse_scale * jnp.dot(coarse_block, again, precision=lax.Precision.HIGHEST)
    iterate = iterate + prolong(second)
    iterate = sweep(iterate)
    iterate = sweep(iterate)
    return (iterate, rhs - fine_op(iterate))


def solution(mesh):
    placed = (
        P(None, "slab", "cross", None),
        P("slab", "cross", None),
        P(),
        P(),
        P(),
        P(),
        P(),
        P(),
        P(),
        P("slab", "cross", None, None),
        P("slab", "cross", None),
    )
    return jax.shard_map(
        local,
        mesh=mesh,
        in_specs=placed,
        out_specs=(P(None, "slab", "cross", None), P(None, "slab", "cross", None)),
        check_vma=False,
    )
```

profile of v0, /device:TPU:34, one launch (start us, length us, event | category | flops | bytes accessed | tf_op | source)
XLA Modules:
  0.0 788.0 jit_solution(14560115293121101571)
XLA Ops:
  8.6 11.8 %gather_fusion = s32[2048]{0:T(1024)S(1)} fusion(s32[2048]{0:T(1024)S(1)} %bitcast.419, s32[2048]{0:T(1024)S(1)} %get-tuple-element.67), kind=kCustom, calls=%fused_computation | custom fusion | bytes 24576 | tf_op jit(solution)/shard_map/gather | solution.py:104
  42.5 14.3 %scatter_custom_fusion = f32[64,4096]{0,1:T(8,128)} fusion(s32[2048]{0:T(1024)S(1)} %bitcast.467, f32[64,2048]{0,1:T(8,128)S(1)} %bitcast.454, s32[2048]{0:T(1024)S(1)} %get-tuple-element.67, f32[]{:T(128)} %constant.19.clone.1), kind=kCustom, calls=%fused_computation.207 | custom fusion | bytes 1048580 | tf_op jit(solution)/shard_map/scatter | solution.py:123
  69.5 11.8 %gather_fusion.2 = s32[2048]{0:T(1024)S(1)} fusion(s32[2048]{0:T(1024)S(1)} %bitcast.421, s32[2048]{0:T(1024)S(1)} %get-tuple-element.63), kind=kCustom, calls=%fused_computation.6 | custom fusion | bytes 24576 | tf_op jit(solution)/shard_map/gather | solution.py:155
  81.4 17.4 %scatter_custom_fusion.1 = f32[64,2048]{0,1:T(8,128)S(1)} fusion(s32[2048]{0:T(1024)S(1)} %get-tuple-element.68, f32[64,4096]{0,1:T(8,128)} %bitcast.448, s32[2048]{0:T(1024)S(1)} %get-tuple-element.106, f32[]{:T(128)} %constant.19.clone.1), kind=kCustom, calls=%fused_computation.205 | custom fusion | bytes 524800 | tf_op jit(solution)/shard_map/scatter | solution.py:132
  117.3 12.6 %gather_fusion.3 = s32[2048]{0:T(1024)S(1)} fusion(s32[128]{0:T(128)S(1)} %sub.225, s32[2048]{0:T(1024)S(1)} %get-tuple-element.105), kind=kCustom, calls=%fused_computation.7 | custom fusion | bytes 24576 | tf_op jit(solution)/shard_map/gather | solution.py:157
  130.0 8.0 %scatter_custom_fusion.4 = s32[2048]{0:T(1024)S(1)} fusion(s32[2048]{0:T(1024)S(1)} %get-tuple-element.64, s32[2048]{0:T(1024)S(1)} %add_subtract_fusion, s32[]{:T(128)} %constant.20.clone.1), kind=kCustom, calls=%fused_computation.671 | custom fusion | bytes 8196 | tf_op jit(solution)/shard_map/scatter | solution.py:159
  138.6 8.2 %scatter_custom_fusion.5 = s32[4096]{0:T(1024)S(1)} fusion(s32[2048]{0:T(1024)S(1)} %get-tuple-element.62, s32[2048]{0:T(1024)} %bitcast.476, s32[]{:T(128)} %constant.20.clone.1), kind=kCustom, calls=%fused_computation.645 | custom fusion | bytes 16896 | tf_op jit(solution)/shard_map/scatter | solution.py:160
  147.6 11.8 %all-to-all-start = ((s32[1,128,32]{2,0,1:T(1,128)}), s32[1,128,32]{2,0,1:T(1,128)S(1)}, u32[]{:S(2)}, u32[]{:S(2)}) async-start(s32[1,128,32]{2,0,1:T(1,128)} %bitcast.91), calls=%async_computation | async-start | bytes 131072 | tf_op jit(solution)/shard_map/all_to_all | solution.py:161
  176.1 8.1 %scatter_custom_fusion.6 = f32[4096]{0:T(1024)S(1)} fusion(s32[2048]{0:T(1024)S(1)} %get-tuple-element.62, f32[2048]{0:T(1024)S(1)} %bitcast.436, f32[]{:T(128)} %constant.19.clone.1), kind=kCustom, calls=%fused_computation.640 | custom fusion | bytes 16388 | tf_op jit(solution)/shard_map/scatter | solution.py:66
  185.5 9.8 %all-to-all-start.1 = ((f32[1,128,32]{2,0,1:T(1,128)}), f32[1,128,32]{2,0,1:T(1,128)S(1)}, u32[]{:S(2)}, u32[]{:S(2)}) async-start(f32[1,128,32]{2,0,1:T(1,128)} %bitcast.92), calls=%async_computation.1 | async-start | bytes 131072 | tf_op jit(solution)/shard_map/all_to_all | solution.py:145
  205.0 29.1 %scatter_custom_fusion.7 = f32[128]{0:T(128)S(1)} fusion(s32[4096]{0:T(1024)} %reshape.754, f32[4096]{0:T(1024)} %reshape.756, f32[]{:T(128)} %constant.62.clone.1), kind=kCustom, calls=%fused_computation.689 | custom fusion | flops 4096 | bytes 1024 | tf_op jit(solution)/shard_map/scatter-add | solution.py:173
  251.2 14.4 %scatter_custom_fusion.2 = f32[64,4096]{0,1:T(8,128)} fusion(s32[2048]{0:T(1024)} %bitcast.469, f32[64,2048]{0,1:T(8,128)S(1)} %bitcast.456, s32[2048]{0:T(1024)} %copy-done.59, f32[]{:T(128)} %constant.19.clone.1), kind=kCustom, calls=%fused_computation.203 | custom fusion | bytes 1049088 | tf_op jit(solution)/shard_map/scatter | solution.py:123
  273.2 17.5 %scatter_custom_fusion.3 = f32[64,2048]{0,1:T(8,128)S(1)} fusion(s32[2048]{0:T(1024)} %copy-done.64, f32[64,4096]{0,1:T(8,128)} %bitcast.450, s32[2048]{0:T(1024)} %copy-done.66, f32[]{:T(128)} %constant.19.clone.1), kind=kCustom, calls=%fused_computation.201 | custom fusion | bytes 524800 | tf_op jit(solution)/shard_map/scatter | solution.py:132
  313.2 6.1 collective-permute-done.8
  336.5 7.4 scatter_custom_fusion.8
  353.0 7.4 all-to-all-done.2
  364.4 28.7 %scatter_custom_fusion.9 = f32[128,8]{1,0:T(8,128)S(1)} fusion(s32[4096]{0:T(1024)} %reshape.754, f32[4096,8]{1,0:T(8,128)} %copy.499, f32[]{:T(128)} %constant.19.clone.1), kind=kCustom, calls=%fused_computation.533 | custom fusion | flops 32768 | bytes 4608 | tf_op jit(solution)/shard_map/scatter-add | solution.py:173
  394.2 15.4 %gather_fusion.4 = f32[4096,8]{1,0:T(8,128)} fusion(f32[8,128]{0,1:T(8,128)S(1)} %copy.500, s32[4096]{0:T(1024)} %broadcast_clamp_fusion), kind=kCustom, calls=%fused_computation.8 | custom fusion | bytes 278528 | tf_op jit(solution)/shard_map/gather | solution.py:176
  412.0 14.2 %all_to_all.30 = f32[128,1,256]{2,1,0:T(1,128)S(1)} all-to-all(f32[128,1,256]{2,1,0:T(1,128)S(1)} %reshape.1035), channel_id=1, replica_groups=mesh['slab'=16,'cross'=8] {'slab','cross'}, dimensions={0} | all-to-all | bytes 262144 | tf_op jit(solution)/shard_map/all_to_all | solution.py:145
  429.3 9.2 %gather_fusion.5 = f32[2048,8]{1,0:T(8,128)} fusion(f32[8,4096]{0,1:T(8,128)} %bitcast.433, s32[2048]{0:T(1024)S(1)} %copy-done.53), kind=kCustom, calls=%fused_computation.9 | custom fusion | bytes 139264 | tf_op jit(solution)/shard_map/gather | solution.py:177
  472.9 7.4 scatter_custom_fusion.10
  482.7 17.5 %all_to_all.31 = f32[128,1,256]{2,1,0:T(1,128)S(1)} all-to-all(f32[128,1,256]{2,1,0:T(1,128)S(1)} %reshape.1037), channel_id=1, replica_groups=mesh['slab'=16,'cross'=8] {'slab','cross'}, dimensions={0} | all-to-all | bytes 262144 | tf_op jit(solution)/shard_map/all_to_all | solution.py:145
  503.7 28.7 %scatter_custom_fusion.11 = f32[128,8]{1,0:T(8,128)S(1)} fusion(s32[4096]{0:T(1024)} %reshape.754, f32[4096,8]{1,0:T(8,128)} %copy.522, f32[]{:T(128)} %constant.19.clone.1), kind=kCustom, calls=%fused_computation.531 | custom fusion | flops 32768 | bytes 4608 | tf_op jit(solution)/shard_map/scatter-add | solution.py:173
  533.4 15.4 %gather_fusion.6 = f32[4096,8]{1,0:T(8,128)} fusion(f32[8,128]{0,1:T(8,128)S(1)} %copy.523, s32[4096]{0:T(1024)} %broadcast_clamp_fusion), kind=kCustom, calls=%fused_computation.10 | custom fusion | bytes 278528 | tf_op jit(solution)/shard_map/gather | solution.py:176
  551.3 14.4 %all_to_all.32 = f32[128,1,256]{2,1,0:T(1,128)S(1)} all-to-all(f32[128,1,256]{2,1,0:T(1,128)S(1)} %reshape.1039), channel_id=1, replica_groups=mesh['slab'=16,'cross'=8] {'slab','cross'}, dimensions={0} | all-to-all | bytes 262144 | tf_op jit(solution)/shard_map/all_to_all | solution.py:145
  570.4 9.2 %gather_fusion.7 = f32[2048,8]{1,0:T(8,128)} fusion(f32[8,4096]{0,1:T(8,128)} %bitcast.434, s32[2048]{0:T(1024)S(1)} %copy-done.54), kind=kCustom, calls=%fused_computation.11 | custom fusion | bytes 139264 | tf_op jit(solution)/shard_map/gather | solution.py:177
  602.3 6.1 collective-permute-done.16
  622.9 18.9 %scatter_custom_fusion.12 = f32[64,4096]{0,1:T(8,128)} fusion(s32[2048]{0:T(1024)} %bitcast.470, f32[64,2048]{0,1:T(8,128)} %bitcast.457, s32[2048]{0:T(1024)} %copy-done.59, f32[]{:T(128)} %constant.19.clone.1), kind=kCustom, calls=%fused_computation.199 | custom fusion | bytes 1049088 | tf_op jit(solution)/shard_map/scatter | solution.py:123
  641.8 6.6 convolution_bitcast_fusion.3
  651.7 18.3 %scatter_custom_fusion.13 = f32[64,2048]{0,1:T(8,128)} fusion(s32[2048]{0:T(1024)} %copy-done.64, f32[64,4096]{0,1:T(8,128)} %bitcast.451, s32[2048]{0:T(1024)} %copy-done.66, f32[]{:T(128)} %constant.19.clone.1), kind=kCustom, calls=%fused_computation.197 | custom fusion | bytes 524800 | tf_op jit(solution)/shard_map/scatter | solution.py:132
  710.5 18.8 %scatter_custom_fusion.14 = f32[64,4096]{0,1:T(8,128)} fusion(s32[2048]{0:T(1024)} %bitcast.471, f32[64,2048]{0,1:T(8,128)} %bitcast.455, s32[2048]{0:T(1024)} %copy-done.59, f32[]{:T(128)} %constant.19.clone.1), kind=kCustom, calls=%fused_computation.195 | custom fusion | bytes 1049088 | tf_op jit(solution)/shard_map/scatter | solution.py:123
  736.9 17.5 %scatter_custom_fusion.15 = f32[64,2048]{0,1:T(8,128)S(1)} fusion(s32[2048]{0:T(1024)} %copy-done.64, f32[64,4096]{0,1:T(8,128)} %bitcast.449, s32[2048]{0:T(1024)} %copy-done.66, f32[]{:T(128)} %constant.19.clone.1), kind=kCustom, calls=%fused_computation.193 | custom fusion | bytes 524800 | tf_op jit(solution)/shard_map/scatter | solution.py:132
  (421 shorter events, 343.2 us)
Async XLA Ops:
  101.8 132.9 %collective-permute-start.3 = (f32[64,1,4,128]{3,0,2,1:T(8,128)}, f32[64,1,4,128]{3,0,2,1:T(8,128)}, u32[]{:S(2)}, u32[]{:S(2)}) collective-permute-start(f32[64,1,4,128]{3,0,2,1:T(8,128)} %get-tuple-element.50), channel_id=1, source_target_pairs={{8,0},{16,8},{24,16},{32,24},{40,32},{48,40},{56,48},{64,56},{72,6... | collective-permute-start | bytes 393224 | tf_op jit(solution)/shard_map/ppermute | solution.py:15
  106.7 128.0 %collective-permute-start.1 = (f32[64,1,4,128]{3,0,2,1:T(8,128)}, f32[64,1,4,128]{3,0,2,1:T(8,128)}, u32[]{:S(2)}, u32[]{:S(2)}) collective-permute-start(f32[64,1,4,128]{3,0,2,1:T(8,128)} %get-tuple-element.49), channel_id=1, source_target_pairs={{0,8},{8,16},{16,24},{24,32},{32,40},{40,48},{48,56},{56,64},{64,7... | collective-permute-start | bytes 393224 | tf_op jit(solution)/shard_map/ppermute | solution.py:14
  108.6 60.3 %collective-permute-start.2 = (f32[1,4,128]{2,1,0:T(4,128)S(1)}, f32[1,4,128]{2,1,0:T(4,128)S(1)}, u32[]{:S(2)}, u32[]{:S(2)}) collective-permute-start(f32[1,4,128]{2,1,0:T(4,128)S(1)} %get-tuple-element.66), channel_id=1, source_target_pairs={{8,0},{16,8},{24,16},{32,24},{40,32},{48,40},{56,48},{64,56},{72,6... | collective-permute-start | bytes 6152 | tf_op jit(solution)/shard_map/ppermute | solution.py:15
  114.6 54.3 %collective-permute-start = (f32[1,4,128]{2,1,0:T(4,128)S(1)}, f32[1,4,128]{2,1,0:T(4,128)S(1)}, u32[]{:S(2)}, u32[]{:S(2)}) collective-permute-start(f32[1,4,128]{2,1,0:T(4,128)S(1)} %get-tuple-element.65), channel_id=1, source_target_pairs={{0,8},{8,16},{16,24},{24,32},{32,40},{40,48},{48,56},{56,64},{64,7... | collective-permute-start | bytes 6152 | tf_op jit(solution)/shard_map/ppermute | solution.py:14
  147.6 37.5 %all-to-all-start = ((s32[1,128,32]{2,0,1:T(1,128)}), s32[1,128,32]{2,0,1:T(1,128)S(1)}, u32[]{:S(2)}, u32[]{:S(2)}) async-start(s32[1,128,32]{2,0,1:T(1,128)} %bitcast.91), calls=%async_computation | async-start | bytes 131072 | tf_op jit(solution)/shard_map/all_to_all | solution.py:161
  169.0 15.9 %collective-permute-start.4 = (f32[6,1,128]{2,1,0:T(1,128)S(1)}, f32[6,1,128]{2,1,0:T(1,128)S(1)}, u32[]{:S(2)}, u32[]{:S(2)}) collective-permute-start(f32[6,1,128]{2,1,0:T(1,128)S(1)} %get-tuple-element.55), channel_id=1, source_target_pairs={{0,1},{1,2},{2,3},{3,4},{4,5},{5,6},{6,7},{8,9},{9,10},{10,11},{11... | collective-permute-start | bytes 9224 | tf_op jit(solution)/shard_map/ppermute | solution.py:14
  171.0 13.9 %collective-permute-start.6 = (f32[6,1,128]{2,1,0:T(1,128)S(1)}, f32[6,1,128]{2,1,0:T(1,128)S(1)}, u32[]{:S(2)}, u32[]{:S(2)}) collective-permute-start(f32[6,1,128]{2,1,0:T(1,128)S(1)} %get-tuple-element.56), channel_id=1, source_target_pairs={{1,0},{2,1},{3,2},{4,3},{5,4},{6,5},{7,6},{9,8},{10,9},{11,10},{12... | collective-permute-start | bytes 9224 | tf_op jit(solution)/shard_map/ppermute | solution.py:15
  185.5 17.4 %all-to-all-start.1 = ((f32[1,128,32]{2,0,1:T(1,128)}), f32[1,128,32]{2,0,1:T(1,128)S(1)}, u32[]{:S(2)}, u32[]{:S(2)}) async-start(f32[1,128,32]{2,0,1:T(1,128)} %bitcast.92), calls=%async_computation.1 | async-start | bytes 131072 | tf_op jit(solution)/shard_map/all_to_all | solution.py:145
  196.6 134.6 %copy-start.36 = (f32[4,4,128]{2,1,0:T(4,128)}, f32[4,4,128]{2,1,0:T(4,128)S(1)}, u32[]{:S(2)}) copy-start(f32[4,4,128]{2,1,0:T(4,128)S(1)} %get-tuple-element.59) | copy-start | bytes 24580
  235.5 8.1 %collective-permute-start.7 = (f32[64,6,1,128]{3,0,2,1:T(8,128)S(1)}, f32[64,6,1,128]{3,0,2,1:T(8,128)S(1)}, u32[]{:S(2)}, u32[]{:S(2)}) collective-permute-start(f32[64,6,1,128]{3,0,2,1:T(8,128)S(1)} %get-tuple-element.38), channel_id=1, source_target_pairs={{1,0},{2,1},{3,2},{4,3},{5,4},{6,5},{7,6},{9,8},{10,9},{11,10},{12... | collective-permute-start | bytes 589832 | tf_op jit(solution)/shard_map/ppermute | solution.py:15
  238.2 7.0 collective-permute-start.5
  304.8 8.3 %collective-permute-start.9 = (f32[64,1,4,128]{3,0,2,1:T(8,128)S(1)}, f32[64,1,4,128]{3,0,2,1:T(8,128)S(1)}, u32[]{:S(2)}, u32[]{:S(2)}) collective-permute-start(f32[64,1,4,128]{3,0,2,1:T(8,128)S(1)} %get-tuple-element.48), channel_id=1, source_target_pairs={{8,0},{16,8},{24,16},{32,24},{40,32},{48,40},{56,48},{64,56},{72,6... | collective-permute-start | bytes 393224 | tf_op jit(solution)/shard_map/ppermute | solution.py:15
  309.2 10.1 %collective-permute-start.8 = (f32[64,1,4,128]{3,0,2,1:T(8,128)S(1)}, f32[64,1,4,128]{3,0,2,1:T(8,128)S(1)}, u32[]{:S(2)}, u32[]{:S(2)}) collective-permute-start(f32[64,1,4,128]{3,0,2,1:T(8,128)S(1)} %get-tuple-element.47), channel_id=1, source_target_pairs={{0,8},{8,16},{16,24},{24,32},{32,40},{40,48},{48,56},{56,64},{64,7... | collective-permute-start | bytes 393224 | tf_op jit(solution)/shard_map/ppermute | solution.py:14
  319.3 6.5 collective-permute-start.11
  322.0 7.1 collective-permute-start.10
  347.0 13.4 %all-to-all-start.2 = ((f32[128,1,256]{2,1,0:T(1,128)}), f32[128,1,256]{2,1,0:T(1,128)S(1)}, u32[]{:S(2)}, u32[]{:S(2)}) async-start(f32[128,1,256]{2,1,0:T(1,128)} %reshape.1033), calls=%async_computation.2 | async-start | bytes 262144 | tf_op jit(solution)/shard_map/all_to_all | solution.py:145
  445.5 9.5 %collective-permute-start.12 = (f32[64,1,4,128]{3,0,2,1:T(8,128)S(1)}, f32[64,1,4,128]{3,0,2,1:T(8,128)S(1)}, u32[]{:S(2)}, u32[]{:S(2)}) collective-permute-start(f32[64,1,4,128]{3,0,2,1:T(8,128)S(1)} %get-tuple-element.46), channel_id=1, source_target_pairs={{0,8},{8,16},{16,24},{24,32},{32,40},{40,48},{48,56},{56,64},{64,7... | collective-permute-start | bytes 393224 | tf_op jit(solution)/shard_map/ppermute | solution.py:14
  447.8 8.4 %collective-permute-start.13 = (f32[64,1,4,128]{3,0,2,1:T(8,128)S(1)}, f32[64,1,4,128]{3,0,2,1:T(8,128)S(1)}, u32[]{:S(2)}, u32[]{:S(2)}) collective-permute-start(f32[64,1,4,128]{3,0,2,1:T(8,128)S(1)} %get-tuple-element.45), channel_id=1, source_target_pairs={{8,0},{16,8},{24,16},{32,24},{40,32},{48,40},{56,48},{64,56},{72,6... | collective-permute-start | bytes 393224 | tf_op jit(solution)/shard_map/ppermute | solution.py:15
  456.2 5.9 collective-permute-start.15
  458.2 7.0 collective-permute-start.14
  594.8 7.5 collective-permute-start.17
  599.1 9.2 %collective-permute-start.16 = (f32[64,1,4,128]{3,0,2,1:T(8,128)S(1)}, f32[64,1,4,128]{3,0,2,1:T(8,128)S(1)}, u32[]{:S(2)}, u32[]{:S(2)}) collective-permute-start(f32[64,1,4,128]{3,0,2,1:T(8,128)S(1)} %get-tuple-element.43), channel_id=1, source_target_pairs={{0,8},{8,16},{16,24},{24,32},{32,40},{40,48},{48,56},{56,64},{64,7... | collective-permute-start | bytes 393224 | tf_op jit(solution)/shard_map/ppermute | solution.py:14
  608.4 6.0 collective-permute-start.19
  610.5 7.1 collective-permute-start.18
  685.1 7.0 collective-permute-start.21
  687.1 9.0 %collective-permute-start.20 = (f32[64,1,4,128]{3,0,2,1:T(8,128)S(1)}, f32[64,1,4,128]{3,0,2,1:T(8,128)S(1)}, u32[]{:S(2)}, u32[]{:S(2)}) collective-permute-start(f32[64,1,4,128]{3,0,2,1:T(8,128)S(1)} %get-tuple-element.41), channel_id=1, source_target_pairs={{0,8},{8,16},{16,24},{24,32},{32,40},{40,48},{48,56},{56,64},{64,7... | collective-permute-start | bytes 393224 | tf_op jit(solution)/shard_map/ppermute | solution.py:14
  696.1 6.2 collective-permute-start.23
  698.1 7.1 collective-permute-start.22
  763.1 6.9 collective-permute-start.25
  765.1 9.0 %collective-permute-start.24 = (f32[64,1,4,128]{3,0,2,1:T(8,128)S(1)}, f32[64,1,4,128]{3,0,2,1:T(8,128)S(1)}, u32[]{:S(2)}, u32[]{:S(2)}) collective-permute-start(f32[64,1,4,128]{3,0,2,1:T(8,128)S(1)} %copy-done.51), channel_id=1, source_target_pairs={{0,8},{8,16},{16,24},{24,32},{32,40},{40,48},{48,56},{56,64},{64,7... | collective-permute-start | bytes 393224 | tf_op jit(solution)/shard_map/ppermute | solution.py:14
  774.1 5.6 collective-permute-start.27
  776.0 7.0 collective-permute-start.26
  (67 other events, 1361.3 us)
where the time goes:
time: 797 us; the launch traced here: 788 us
  local copies, waits for them, and re-layouts  325 us (41%)
  other arithmetic  144 us (18%)
  matrix products  113 us (14%)
  starting transfers between devices  108 us (14%)
  waiting for transfers between devices  48.3 us (6%)
  blocking collectives  46.1 us (6%)
    scatter-add x3, other arithmetic, to_owner(): return jax.ops.segment_sum(arrived.T, received_ids, agg_count).T  86.5 us
    dot_general x78, matrix products, apply_block(): jnp.einsum('ij,jabc->iabc', matrix, field, precision=lax.Precision.HIGHEST)  75.9 us
    scatter x8, local copies, waits for them, and re-layouts, smooth(): update = jnp.zeros((node_count, element_count), jnp.float32).at[:, class_...  75.6 us
    scatter x4, local copies, waits for them, and re-layouts, smooth(): bucket = jnp.zeros((node_count, tile_count * tile_width), jnp.float32).at...  66.4 us
    all_to_all x3, blocking collectives, move_floats(): lax.all_to_all(buffer, ('slab', 'cross'), split_axis=1, concat_axis=1, ti...  46.1 us
    ppermute x14, starting transfers between devices, with_halo(): after = lax.ppermute(initial, axis, down)  45.9 us
    ppermute x14, starting transfers between devices, with_halo(): before = lax.ppermute(last, axis, up)  35.1 us
    ppermute x14, waiting for transfers between devices, with_halo(): before = lax.ppermute(last, axis, up)  33.7 us
  transfers between devices with their start and end apart: 31, of which 16 were waited for; matrix products, arithmetic and copies ran while one was open for 13% of the time, Pallas kernels for 0%

commit v1 on v0

v1 whole, which is shorter than its diff:
```python
import functools

import jax
import jax.numpy as jnp
from jax import lax
from jax.experimental import pallas as pl
from jax.experimental.pallas import tpu as pltpu
from jax.sharding import PartitionSpec as P

MESH = pl.DeviceIdType.MESH
F32 = jnp.float32
BF16 = jnp.bfloat16
HIGHEST = lax.Precision.HIGHEST
LANES = 128
WIDE = 4
NT = (((1,), (1,)), ((), ()))


def dot(a, b):
    return jnp.dot(a, b, preferred_element_type=F32)


def dot_nt(a, b):
    return lax.dot_general(a, b, NT, preferred_element_type=F32)


def parts(value):
    high = value.astype(BF16).astype(F32)
    return high, value - high


def stack_rows(value):
    high, low = parts(value)
    pieces = [high, low, high]
    if value.shape[0] == 8:
        pieces.append(jnp.zeros_like(value))
    return jnp.concatenate(pieces, axis=0).astype(BF16)


def stack_columns(value):
    high, low = parts(value)
    pieces = [high, high, low]
    if value.shape[1] == 8:
        pieces.append(jnp.zeros_like(value))
    return jnp.concatenate(pieces, axis=1).astype(BF16)


def cycle(
    n_slab,
    n_cross,
    cap,
    rhs_ref,
    class_ref,
    perm_ref,
    vol_ref,
    side_ref,
    couple_ref,
    smooth_ref,
    restrict_ref,
    coarse_ref,
    owner_ref,
    local_ref,
    sol_ref,
    res_ref,
    rs,
    halo_rhs,
    fields,
    halos,
    start_field,
    fine_res,
    acc,
    gx0,
    gx1,
    gy0,
    gy1,
    blocks_f32,
    op_stack,
    smooth_stack,
    prolong_stack,
    coarse_stack,
    perm_b,
    perm_inv,
    weights,
    owner_hot,
    rank_b,
    packed,
    local_hot,
    mail,
    coarse_keep,
    coarse_field,
    halo_coarse,
    halo_send,
    halo_recv,
    mail_send,
    mail_recv,
):
    s, c = lax.axis_index("slab"), lax.axis_index("cross")
    owners = n_slab * n_cross
    s_up, s_down = lax.rem(s + 1, n_slab), lax.rem(s + n_slab - 1, n_slab)
    c_up, c_down = lax.rem(c + 1, n_cross), lax.rem(c + n_cross - 1, n_cross)
    lane = lax.broadcasted_iota(jnp.int32, (8, LANES), 1)

    barrier = pltpu.get_barrier_semaphore()

    def greet_slab(off, carry):
        pl.semaphore_signal(
            barrier, inc=1, device_id=(lax.rem(s + off, n_slab), c), device_id_type=MESH
        )
        return carry

    def greet_cross(off, carry):
        pl.semaphore_signal(
            barrier, inc=1, device_id=(s, lax.rem(c + off, n_cross)), device_id_type=MESH
        )
        return carry

    lax.fori_loop(1, n_slab, greet_slab, 0)
    lax.fori_loop(1, n_cross, greet_cross, 0)

    for xy in range(WIDE * WIDE):
        x, y = xy // WIDE, xy % WIDE
        rs[x, y, 0:64, :] = rhs_ref[pl.ds(xy, 64, stride=WIDE * WIDE), :]
        rs[x, y, 64:72, :] = jnp.broadcast_to(class_ref[xy : xy + 1, :], (8, LANES)).astype(F32)

    pl.semaphore_wait(barrier, n_slab + n_cross - 2)

    def halo_copies(source, target, turn):
        plan = (
            (source.at[0], 1, (s_down, c)),
            (source.at[WIDE - 1], 0, (s_up, c)),
            (source.at[:, 0], 3, (s, c_down)),
            (source.at[:, WIDE - 1], 2, (s, c_up)),
        )
        return [
            pltpu.make_async_remote_copy(
                src_ref=face,
                dst_ref=target.at[side],
                send_sem=halo_send.at[turn, side],
                recv_sem=halo_recv.at[turn, side],
                device_id=device,
                device_id_type=MESH,
            )
            for face, side, device in plan
        ]

    def send_halo(source, target, turn):
        for copy in halo_copies(source, target, turn):
            copy.start()

    def await_halo(source, target, turn):
        for copy in halo_copies(source, target, turn):
            copy.wait_recv()

    send_halo(rs, halo_rhs, 0)

    blocks_f32[0:64, :] = vol_ref[...]
    blocks_f32[64:448, :] = side_ref[...]
    for m in range(3):
        plus = couple_ref[m * 64 : (m + 1) * 64, :]
        blocks_f32[448 + 128 * m : 512 + 128 * m, :] = plus.T
        blocks_f32[512 + 128 * m : 576 + 128 * m, :] = plus
    blocks_f32[832:896, :] = jnp.where(
        lax.broadcasted_iota(jnp.int32, (64, 64), 0) == lax.broadcasted_iota(jnp.int32, (64, 64), 1),
        1.0,
        0.0,
    )
    for m in range(13):
        rows = slice(64 * m, 64 * m + 64)
        op_stack[rows, :] = stack_columns(blocks_f32[rows, :])
    for m in range(16):
        rows = slice(64 * m, 64 * m + 64)
        smooth_stack[rows, :] = stack_columns(smooth_ref[rows, :])
    restrict = restrict_ref[...]
    short = lax.dot_general(
        blocks_f32[...], restrict, NT, precision=HIGHEST, preferred_element_type=F32
    )
    prolong_stack[...] = stack_columns(short)
    tiny = [
        jnp.dot(restrict, short[64 * m : 64 * m + 64], precision=HIGHEST, preferred_element_type=F32)
        for m in range(13)
    ]
    coarse_stack[...] = stack_columns(jnp.concatenate(tiny + [jnp.zeros((8, 8), F32)], axis=0))
    restrict_cols = stack_columns(jnp.concatenate([restrict, jnp.zeros_like(restrict)], axis=0))

    hot_rows = lax.broadcasted_iota(jnp.int32, (owners, LANES), 0)
    before = jnp.concatenate(
        [
            jnp.where(
                lax.broadcasted_iota(jnp.int32, (LANES, LANES), 0)
                < lax.broadcasted_iota(jnp.int32, (LANES, LANES), 1),
                1.0,
                0.0,
            ),
            jnp.ones((LANES, LANES), F32),
        ],
        axis=1,
    ).astype(BF16)
    seen = jnp.zeros((owners, LANES), F32)
    for xy in range(WIDE * WIDE):
        x, y = xy // WIDE, xy % WIDE
        hot = jnp.where(hot_rows == owner_ref[xy : xy + 1, :], 1.0, 0.0)
        hot_low = hot.astype(BF16)
        owner_hot[0:owners, xy * LANES : (xy + 1) * LANES] = hot_low
        owner_hot[owners : 2 * owners, xy * LANES : (xy + 1) * LANES] = hot_low
        counted = dot(hot_low, before)
        rank = jnp.sum(hot * (counted[:, 0:LANES] + seen), axis=0, keepdims=True)
        seen = seen + counted[:, LANES : 2 * LANES]
        rank_b[x, y] = jnp.broadcast_to(rank, (8, LANES))

    def perm_of(label):
        value = jnp.zeros_like(label)
        for k in range(16):
            value = jnp.where(label == float(k), perm_ref[k], value)
        return value

    def own_perm(x, carry):
        for y in range(WIDE):
            value = perm_of(rs[x, y, 64:72, :])
            perm_b[x, y] = value
            perm_inv[x, y] = 1.0 / value
        return carry

    lax.fori_loop(0, WIDE, own_perm, 0)

    def slab_copy(turn, source, target, off, stage):
        to = lax.rem(s + off, n_slab)
        return pltpu.make_async_remote_copy(
            src_ref=mail.at[turn, source, :, pl.ds(pl.multiple_of(to * n_cross, n_cross), n_cross)],
            dst_ref=mail.at[turn, target, :, pl.ds(pl.multiple_of(s * n_cross, n_cross), n_cross)],
            send_sem=mail_send.at[turn, stage],
            recv_sem=mail_recv.at[turn, stage],
            device_id=(to, c),
            device_id_type=MESH,
        )

    def cross_copy(turn, source, target, off, stage):
        to = lax.rem(c + off, n_cross)
        return pltpu.make_async_remote_copy(
            src_ref=mail.at[turn, source, :, pl.ds(pl.multiple_of(to * n_slab, n_slab), n_slab)],
            dst_ref=mail.at[turn, target, :, pl.ds(pl.multiple_of(c * n_slab, n_slab), n_slab)],
            send_sem=mail_send.at[turn, stage],
            recv_sem=mail_recv.at[turn, stage],
            device_id=(s, to),
            device_id_type=MESH,
        )

    def post(turn, source, target, stage, along_slab):
        def one(off, carry):
            (slab_copy if along_slab else cross_copy)(turn, source, target, off, stage).start()
            return carry

        lax.fori_loop(1, n_slab if along_slab else n_cross, one, 0)
        size, place = (n_cross, s) if along_slab else (n_slab, c)
        rows = pl.ds(pl.multiple_of(place * size, size), size)
        mail[turn, target, :, rows, :] = mail[turn, source, :, rows, :]

    def rows_moved(along_slab):
        return (n_slab - 1) * n_cross if along_slab else (n_cross - 1) * n_slab

    def collect(turn, target, stage, along_slab):
        part = mail.at[turn, target, :, pl.ds(0, rows_moved(along_slab))]
        pltpu.make_async_copy(part, part, mail_recv.at[turn, stage]).wait()

    def release(turn, source, stage, along_slab):
        part = mail.at[turn, source, :, pl.ds(0, rows_moved(along_slab))]
        pltpu.make_async_copy(part, part, mail_send.at[turn, stage]).wait()

    def write_mail(turn, value):
        for h in range(cap // 16):
            mail[turn, 0, h] = value[:, h * LANES : (h + 1) * LANES]

    def read_mail(turn):
        return jnp.concatenate([mail[turn, 3, h].T for h in range(cap // 16)], axis=0)

    def pack(load):
        def one(x, carry):
            for y in range(WIDE):
                rank = rank_b[x, y]
                keep = [rank == float(r) for r in range(cap)]
                columns = pl.ds(pl.multiple_of((x * WIDE + y) * LANES, LANES), LANES)
                for i, piece in enumerate(parts(load(x, y))):
                    spread = jnp.concatenate([jnp.where(k, piece, 0.0) for k in keep], axis=0)
                    packed[i * cap * 8 : (i + 1) * cap * 8, columns] = spread.astype(BF16)
            return carry

        lax.fori_loop(0, WIDE, one, 0)

    def to_owner_start(turn, load):
        pack(load)
        slots = dot_nt(owner_hot[0:owners, :], packed[...])
        write_mail(turn, slots[:, 0 : cap * 8] + slots[:, cap * 8 : 2 * cap * 8])
        post(turn, 0, 1, 0, True)

    def to_owner_middle(turn):
        collect(turn, 1, 0, True)
        for k in range(n_cross):
            for h in range(cap // 16):
                mail[turn, 2, h, k * n_slab : (k + 1) * n_slab, :] = mail[
                    turn, 1, h, pl.ds(k, n_slab, stride=n_cross), :
                ]
        post(turn, 2, 3, 1, False)

    def to_owner_end(turn):
        collect(turn, 3, 1, False)
        return read_mail(turn)

    def gather_sum(arrived):
        flat = jnp.concatenate([arrived[8 * r : 8 * r + 8] for r in range(cap)], axis=1)
        high, low = parts(flat)
        both = dot_nt(jnp.concatenate([high, low], axis=0).astype(BF16), local_hot[...])
        return both[0:8] + both[8:16]

    def from_owner_start(turn, value):
        high, low = parts(value)
        both = dot(jnp.concatenate([high, low], axis=0).astype(BF16), local_hot[...])
        flat = both[0:8] + both[8:16]
        out = jnp.concatenate([flat[:, owners * r : owners * (r + 1)] for r in range(cap)], axis=0)
        write_mail(turn, out.T)
        post(turn, 0, 1, 0, False)

    def from_owner_middle(turn):
        collect(turn, 1, 0, False)
        for k in range(n_slab):
            for h in range(cap // 16):
                mail[turn, 2, h, k * n_cross : (k + 1) * n_cross, :] = mail[
                    turn, 1, h, pl.ds(k, n_cross, stride=n_slab), :
                ]
        post(turn, 2, 3, 1, True)

    def from_owner_end(turn, target):
        collect(turn, 3, 1, True)
        high, low = parts(read_mail(turn))
        spread = jnp.concatenate([high, low], axis=1).astype(BF16)
        for pair in range(WIDE * WIDE // 2):
            both = dot(spread, owner_hot[:, pair * 2 * LANES : (pair + 1) * 2 * LANES])
            for i in range(2):
                x, y = (2 * pair + i) // WIDE, (2 * pair + i) % WIDE
                rank = rank_b[x, y]
                value = jnp.zeros((8, LANES), F32)
                for r in range(cap):
                    value = jnp.where(
                        rank == float(r),
                        both[8 * r : 8 * r + 8, i * LANES : (i + 1) * LANES],
                        value,
                    )
                coarse_field[target, x, y] = value

    def own_products(load, stack, rows, extra=None):
        def one(x, carry):
            for half in range(2):
                ys = (2 * half, 2 * half + 1)
                product = dot(stack[...], jnp.concatenate([load(x, y) for y in ys], axis=1))
                for i, y in enumerate(ys):

                    def block(b):
                        return product[b * rows : (b + 1) * rows, i * LANES : (i + 1) * LANES]

                    def scaled(weight, value):
                        return weight[None] * value.reshape(rows // 8, 8, LANES)

                    total = scaled(perm_b[x, y], block(0))
                    for d in range(6):
                        total = total + scaled(weights[d, x, y], block(1 + d))
                    total = total - scaled(weights[10, x, y], pltpu.roll(block(11), 1, 1))
                    total = total - scaled(weights[11, x, y], pltpu.roll(block(12), LANES - 1, 1))
                    acc[x, y, 0:rows, :] = total.reshape(rows, LANES)
                    gx0[x + 1, y, 0:rows, :] = block(7)
                    gx1[x, y, 0:rows, :] = block(8)
                    gy0[x, y + 1, 0:rows, :] = block(9)
                    gy1[x, y, 0:rows, :] = block(10)
                    if extra is not None:
                        extra(x, y, block(13))
            return carry

        lax.fori_loop(0, WIDE, one, 0)

    def halo_products(load, stack, rows):
        for side in range(4):
            data = jnp.concatenate([load(side, j) for j in range(WIDE)], axis=1)
            if rows == 64:
                product = dot(stack[(7 + side) * rows : (8 + side) * rows, :], data)
            else:
                product = dot(stack[...], data)[(7 + side) * rows : (8 + side) * rows]
            for j in range(WIDE):
                value = product[:, j * LANES : (j + 1) * LANES]
                if side == 0:
                    gx0[0, j, 0:rows, :] = value
                elif side == 1:
                    gx1[WIDE, j, 0:rows, :] = value
                elif side == 2:
                    gy0[j, 0, 0:rows, :] = value
                else:
                    gy1[j, WIDE, 0:rows, :] = value

    def applied(x, y, rows):
        def scaled(weight, value):
            return weight[None] * value.reshape(rows // 8, 8, LANES)

        total = acc[x, y, 0:rows, :].reshape(rows // 8, 8, LANES)
        total = total - scaled(weights[6, x, y], gx0[x, y, 0:rows, :])
        total = total - scaled(weights[7, x, y], gx1[x + 1, y, 0:rows, :])
        total = total - scaled(weights[8, x, y], gy0[x, y, 0:rows, :])
        total = total - scaled(weights[9, x, y], gy1[x, y + 1, 0:rows, :])
        return total.reshape(rows, LANES)

    def smoothed(values, labels, inverses):
        product = dot(smooth_stack[...], jnp.concatenate([stack_rows(v) for v in values], axis=1))
        results = []
        for i, (label, inverse) in enumerate(zip(labels, inverses)):
            columns = slice(i * LANES, (i + 1) * LANES)
            value = product[0:64, columns].reshape(8, 8, LANES)
            for k in range(1, 16):
                block = product[64 * k : 64 * k + 64, columns].reshape(8, 8, LANES)
                value = jnp.where((label == float(k))[None], block, value)
            results.append((value * inverse[None]).reshape(64, LANES))
        return results

    def label_of(x, y):
        return rs[x, y, 64:72, :]

    def first_sweep(x, carry):
        for half in range(2):
            ys = (2 * half, 2 * half + 1)
            found = smoothed(
                [rs[x, y, 0:64, :] for y in ys],
                [label_of(x, y) for y in ys],
                [perm_inv[x, y] for y in ys],
            )
            for y, value in zip(ys, found):
                start_field[x, y] = value
        return carry

    lax.fori_loop(0, WIDE, first_sweep, 0)

    def keys(x, y):
        row = lax.broadcasted_iota(jnp.int32, (8, LANES), 0)
        label = jnp.broadcast_to(local_ref[pl.ds(x * WIDE + y, 1), :], (8, LANES)).astype(F32) + 1.0
        return jnp.where(row == 0, label, jnp.where(row == 1, perm_b[x, y], 0.0))

    to_owner_start(0, keys)

    await_halo(rs, halo_rhs, 0)
    inside = (s > 0, s < n_slab - 1, c > 0, c < n_cross - 1)

    def halo_sweep(side, carry):
        label = [halo_rhs[side, j, 64:72, :] for j in range(WIDE)]
        found = [perm_of(v) for v in label]
        for j in range(WIDE):
            halo_coarse[0, side, j] = found[j]
        for half in range(2):
            js = (2 * half, 2 * half + 1)
            values = smoothed(
                [halo_rhs[side, j, 0:64, :] for j in js],
                [label[j] for j in js],
                [1.0 / found[j] for j in js],
            )
            for j, value in zip(js, values):
                halos[3, side, j] = value
        return carry

    lax.fori_loop(0, 4, halo_sweep, 0)

    for x in range(WIDE):
        for y in range(WIDE):
            own = perm_b[x, y]

            def rim(side, j):
                return jnp.where(inside[side], halo_coarse[0, side, j], 0.0)

            beside = (
                perm_b[x - 1, y] if x > 0 else rim(0, y),
                perm_b[x + 1, y] if x < WIDE - 1 else rim(1, y),
                perm_b[x, y - 1] if y > 0 else rim(2, x),
                perm_b[x, y + 1] if y < WIDE - 1 else rim(3, x),
                jnp.where(lane > 0, pltpu.roll(own, 1, 1), 0.0),
                jnp.where(lane < LANES - 1, pltpu.roll(own, LANES - 1, 1), 0.0),
            )
            there = (
                True if x > 0 else inside[0],
                True if x < WIDE - 1 else inside[1],
                True if y > 0 else inside[2],
                True if y < WIDE - 1 else inside[3],
                lane > 0,
                lane < LANES - 1,
            )
            for d in range(6):
                kn = beside[d]
                w = jnp.where(kn > 0.0, 2.0 * own * kn / (own + kn), 2.0 * own)
                weights[d, x, y] = w
                weights[6 + d, x, y] = w if there[d] is True else jnp.where(there[d], w, 0.0)

    def fine_stack(ref, *lead):
        return lambda x, y: stack_rows(ref[(*lead, x, y)])

    own_products(fine_stack(start_field), op_stack, 64)
    halo_products(fine_stack(halos, 3), op_stack, 64)
    to_owner_middle(0)

    def sweep(residue, iterate, target):
        def one(x, carry):
            for half in range(2):
                ys = (2 * half, 2 * half + 1)
                found = smoothed(
                    [residue(x, y) for y in ys],
                    [label_of(x, y) for y in ys],
                    [perm_inv[x, y] for y in ys],
                )
                for y, value in zip(ys, found):
                    fields[target, x, y] = iterate(x, y) + value
            return carry

        lax.fori_loop(0, WIDE, one, 0)

    sweep(
        lambda x, y: rs[x, y, 0:64, :] - applied(x, y, 64), lambda x, y: start_field[x, y], 0
    )
    send_halo(fields.at[0], halos.at[0], 1)
    own_products(fine_stack(fields, 0), op_stack, 64)

    arrived = to_owner_end(0)
    hot_ids = lax.broadcasted_iota(jnp.int32, (LANES, owners), 0).astype(F32) + 1.0
    for r in range(cap):
        local_hot[:, r * owners : (r + 1) * owners] = jnp.where(
            hot_ids == arrived[8 * r : 8 * r + 1, :], 1.0, 0.0
        ).astype(BF16)
    perm_sum = gather_sum(arrived)[1:2, :]
    coarse_keep[0] = jnp.broadcast_to(1.0 / (1.0 + perm_sum), (8, LANES))

    await_halo(fields.at[0], halos.at[0], 1)
    halo_products(fine_stack(halos, 0), op_stack, 64)

    def second_residue(x, carry):
        rest = []
        for y in range(WIDE):
            value = rs[x, y, 0:64, :] - applied(x, y, 64)
            fine_res[x, y] = value
            rest.append(stack_rows(value))
        found = dot(restrict_cols, jnp.concatenate(rest, axis=1))
        for y in range(WIDE):
            coarse_field[2, x, y] = found[0:8, y * LANES : (y + 1) * LANES]
        return carry

    lax.fori_loop(0, WIDE, second_residue, 0)

    def coarse_step(value):
        product = jnp.dot(
            coarse_ref[...], value, precision=HIGHEST, preferred_element_type=F32
        )
        return coarse_keep[0] * product

    to_owner_start(1, lambda x, y: coarse_field[2, x, y])
    to_owner_middle(1)
    coarse_res = gather_sum(to_owner_end(1))
    first = coarse_step(coarse_res)
    from_owner_start(3, first)
    from_owner_middle(3)
    from_owner_end(3, 0)
    send_halo(coarse_field.at[0], halo_coarse.at[1], 2)
    own_products(fine_stack(coarse_field, 0), coarse_stack, 8)
    await_halo(coarse_field.at[0], halo_coarse.at[1], 2)
    halo_products(fine_stack(halo_coarse, 1), coarse_stack, 8)
    to_owner_start(2, lambda x, y: applied(x, y, 8))
    to_owner_middle(2)
    again = coarse_res - gather_sum(to_owner_end(2))
    second = first + coarse_step(again)
    from_owner_start(4, second)
    from_owner_middle(4)
    from_owner_end(4, 1)
    send_halo(coarse_field.at[1], halo_coarse.at[2], 3)

    def add_prolonged(x, y, value):
        start_field[x, y] = fields[0, x, y] + value

    own_products(fine_stack(coarse_field, 1), prolong_stack, 64, add_prolonged)
    await_halo(coarse_field.at[1], halo_coarse.at[2], 3)
    halo_products(fine_stack(halo_coarse, 2), prolong_stack, 64)
    sweep(lambda x, y: fine_res[x, y] - applied(x, y, 64), lambda x, y: start_field[x, y], 1)
    send_halo(fields.at[1], halos.at[1], 4)

    own_products(fine_stack(fields, 1), op_stack, 64)
    await_halo(fields.at[1], halos.at[1], 4)
    halo_products(fine_stack(halos, 1), op_stack, 64)
    sweep(
        lambda x, y: rs[x, y, 0:64, :] - applied(x, y, 64), lambda x, y: fields[1, x, y], 2
    )
    send_halo(fields.at[2], halos.at[2], 5)
    own_products(fine_stack(fields, 2), op_stack, 64)
    for xy in range(WIDE * WIDE):
        sol_ref[pl.ds(xy, 64, stride=WIDE * WIDE), :] = fields[2, xy // WIDE, xy % WIDE]
    await_halo(fields.at[2], halos.at[2], 5)
    halo_products(fine_stack(halos, 2), op_stack, 64)
    for xy in range(WIDE * WIDE):
        x, y = xy // WIDE, xy % WIDE
        res_ref[pl.ds(xy, 64, stride=WIDE * WIDE), :] = rs[x, y, 0:64, :] - applied(x, y, 64)

    sent = (
        (rs, halo_rhs, 0),
        (fields.at[0], halos.at[0], 1),
        (coarse_field.at[0], halo_coarse.at[1], 2),
        (coarse_field.at[1], halo_coarse.at[2], 3),
        (fields.at[1], halos.at[1], 4),
        (fields.at[2], halos.at[2], 5),
    )
    for source, target, turn in sent:
        for copy in halo_copies(source, target, turn):
            copy.wait_send()
    for turn in range(5):
        release(turn, 0, 0, turn < 3)
        release(turn, 2, 1, turn >= 3)


def local(
    n_slab,
    n_cross,
    cap,
    rhs,
    classes,
    perm,
    vol_block,
    side_blocks,
    couple,
    smoother_blocks,
    restrict_map,
    coarse_block,
    owners,
    agg_local,
):
    vmem = pl.BlockSpec(memory_space=pltpu.VMEM)
    smem = pl.BlockSpec(memory_space=pltpu.SMEM)
    count = n_slab * n_cross
    face = (WIDE, WIDE)
    flat = jax.ShapeDtypeStruct((64 * WIDE * WIDE, LANES), F32)
    scratch = [
        pltpu.VMEM((*face, 72, LANES), F32),
        pltpu.VMEM((4, WIDE, 72, LANES), F32),
        pltpu.VMEM((3, *face, 64, LANES), F32),
        pltpu.VMEM((4, 4, WIDE, 64, LANES), F32),
        pltpu.VMEM((*face, 64, LANES), F32),
        pltpu.VMEM((*face, 64, LANES), F32),
        pltpu.VMEM((*face, 64, LANES), F32),
        pltpu.VMEM((WIDE + 1, WIDE, 64, LANES), F32),
        pltpu.VMEM((WIDE + 1, WIDE, 64, LANES), F32),
        pltpu.VMEM((WIDE, WIDE + 1, 64, LANES), F32),
        pltpu.VMEM((WIDE, WIDE + 1, 64, LANES), F32),
        pltpu.VMEM((14 * 64, 64), F32),
        pltpu.VMEM((13 * 64, 192), BF16),
        pltpu.VMEM((16 * 64, 192), BF16),
        pltpu.VMEM((14 * 64, 32), BF16),
        pltpu.VMEM((14 * 8, 32), BF16),
        pltpu.VMEM((*face, 8, LANES), F32),
        pltpu.VMEM((*face, 8, LANES), F32),
        pltpu.VMEM((12, *face, 8, LANES), F32),
        pltpu.VMEM((2 * count, WIDE * WIDE * LANES), BF16),
        pltpu.VMEM((*face, 8, LANES), F32),
        pltpu.VMEM((2 * cap * 8, WIDE * WIDE * LANES), BF16),
        pltpu.VMEM((LANES, cap * count), BF16),
        pltpu.VMEM((5, 4, cap // 16, count, LANES), F32),
        pltpu.VMEM((1, 8, LANES), F32),
        pltpu.VMEM((3, *face, 8, LANES), F32),
        pltpu.VMEM((3, 4, WIDE, 8, LANES), F32),
        pltpu.SemaphoreType.DMA((6, 4)),
        pltpu.SemaphoreType.DMA((6, 4)),
        pltpu.SemaphoreType.DMA((5, 2)),
        pltpu.SemaphoreType.DMA((5, 2)),
    ]
    flops = 2 * 2048 * (5 * 832 + 5 * 1024) * 192
    solved, residue = pl.pallas_call(
        functools.partial(cycle, n_slab, n_cross, cap),
        out_shape=(flat, flat),
        in_specs=[vmem, vmem, smem] + [vmem] * 8,
        out_specs=(vmem, vmem),
        scratch_shapes=scratch,
        compiler_params=pltpu.CompilerParams(
            collective_id=0, has_side_effects=True, vmem_limit_bytes=56 * 1024 * 1024
        ),
        cost_estimate=pl.CostEstimate(flops=flops, bytes_accessed=4 << 20, transcendentals=0),
    )(
        rhs.reshape(64 * WIDE * WIDE, LANES),
        classes.reshape(WIDE * WIDE, LANES),
        perm,
        vol_block,
        side_blocks.reshape(6 * 64, 64),
        couple.reshape(3 * 64, 64),
        smoother_blocks.reshape(16 * 64, 64),
        restrict_map,
        coarse_block,
        owners.reshape(WIDE * WIDE, LANES),
        agg_local.reshape(WIDE * WIDE, LANES),
    )
    return solved.reshape(rhs.shape), residue.reshape(rhs.shape)


def solution(mesh, cap=32):
    placed = (
        P(None, "slab", "cross", None),
        P("slab", "cross", None),
        P(),
        P(),
        P(),
        P(),
        P(),
        P(),
        P(),
        P("slab", "cross", None, None),
        P("slab", "cross", None),
    )
    return jax.shard_map(
        functools.partial(local, mesh.shape["slab"], mesh.shape["cross"], cap),
        mesh=mesh,
        in_specs=placed,
        out_specs=(P(None, "slab", "cross", None), P(None, "slab", "cross", None)),
        check_vma=False,
    )
```

time: 797 us -> 102 us (0.13)
  the two profiles are of different devices: /device:TPU:34 before, /device:TPU:0 now
where the time goes in v1:
time: 102 us
  Pallas kernels  98.5 us (97%)
  local copies, waits for them, and re-layouts  2.72 us (3%)
    pallas_call x1, Pallas kernels, local(): pl.pallas_call(functools.partial(cycle, n_slab, n_cross, cap), out_shape=...  98.5 us
    unnamed x4, local copies, waits for them, and re-layouts  2.72 us

profile of v1, /device:TPU:0, one launch (start us, length us, event | category | flops | bytes accessed | tf_op | source)
XLA Modules:
  0.0 101.8 jit_solution(10231340756932631438)
XLA Ops:
  0.6 98.5 %shard_map.122 = (f32[1024,128]{1,0:T(8,128)}, f32[1024,128]{1,0:T(8,128)}) custom-call(f32[1024,128]{1,0:T(8,128)} %bitcast.11, s32[16,128]{1,0:T(8,128)} %bitcast.15, f32[16]{0:T(128)} %perm_ref.1, f32[64,64]{1,0:T(8,128)} %vol_ref.1, f32[384,64]{1,0:T(8,128)} %bitcast.13, f32[192,64]{1,0:T(8,128)} %bitcast.14, f32[1024,64]{1,0:T(8,128)} %bitcast.12, ...), custom_call_target="tpu_custom_call" | custom-call | flops 7298088960 | bytes 4194304 | tf_op jit(solution)/shard_map/pallas_call | solution.py:667
  99.1 0.0 copy-start
  99.1 1.9 %copy.15 = f32[64,4,4,128]{3,2,1,0:T(4,128)} copy(f32[64,4,4,128]{3,2,1,0:T(4,128)} %bitcast.10) | data formatting | bytes 1048576
  101.0 0.0 copy-done
  101.0 0.8 copy.16
Async XLA Ops:
  99.1 1.9 %copy-start = (f32[1024,128]{1,0:T(8,128)S(1)}, f32[1024,128]{1,0:T(8,128)}, u32[]{:S(2)}) copy-start(f32[1024,128]{1,0:T(8,128)} %get-tuple-element.5) | copy-start | bytes 1572868

commit v2 on v1

--- a/solution.py
+++ b/solution.py
@@ -49,6 +49,19 @@
     n_slab,
     n_cross,
     cap,
+    rhs_hbm,
+    class_hbm,
+    perm_hbm,
+    vol_hbm,
+    side_hbm,
+    couple_hbm,
+    smooth_hbm,
+    restrict_hbm,
+    coarse_hbm,
+    owner_hbm,
+    local_hbm,
+    sol_ref,
+    res_ref,
     rhs_ref,
     class_ref,
     perm_ref,
@@ -60,10 +73,11 @@
     coarse_ref,
     owner_ref,
     local_ref,
-    sol_ref,
-    res_ref,
+    out_ref,
     rs,
     halo_rhs,
+    label,
+    halo_label,
     fields,
     halos,
     start_field,
@@ -89,10 +103,12 @@
     coarse_keep,
     coarse_field,
     halo_coarse,
+    load_sem,
     halo_send,
     halo_recv,
     mail_send,
     mail_recv,
+    all_here,
 ):
     s, c = lax.axis_index("slab"), lax.axis_index("cross")
     owners = n_slab * n_cross
@@ -117,12 +133,41 @@
     lax.fori_loop(1, n_slab, greet_slab, 0)
     lax.fori_loop(1, n_cross, greet_cross, 0)
 
+    loads = [
+        pltpu.make_async_copy(source, target, load_sem.at[k])
+        for k, (source, target) in enumerate(
+            (
+                (rhs_hbm, rhs_ref),
+                (class_hbm, class_ref),
+                (perm_hbm, perm_ref),
+                (vol_hbm, vol_ref),
+                (side_hbm, side_ref),
+                (couple_hbm, couple_ref),
+                (smooth_hbm, smooth_ref),
+                (restrict_hbm, restrict_ref),
+                (coarse_hbm, coarse_ref),
+                (owner_hbm, owner_ref),
+                (local_hbm, local_ref),
+            )
+        )
+    ]
+    for copy in loads:
+        copy.start()
+    loads[0].wait()
+    loads[1].wait()
+
     for xy in range(WIDE * WIDE):
         x, y = xy // WIDE, xy % WIDE
-        rs[x, y, 0:64, :] = rhs_ref[pl.ds(xy, 64, stride=WIDE * WIDE), :]
-        rs[x, y, 64:72, :] = jnp.broadcast_to(class_ref[xy : xy + 1, :], (8, LANES)).astype(F32)
+        rs[x, y] = rhs_ref[pl.ds(xy, 64, stride=WIDE * WIDE), :]
+        label[x, y] = jnp.broadcast_to(class_ref[xy : xy + 1, :], (8, LANES)).astype(F32)
 
     pl.semaphore_wait(barrier, n_slab + n_cross - 2)
+
+    sent = []
+
+    def drain():
+        for finish in sent:
+            finish()
 
     def halo_copies(source, target, turn):
         plan = (
@@ -146,12 +191,24 @@
     def send_halo(source, target, turn):
         for copy in halo_copies(source, target, turn):
             copy.start()
+            sent.append(copy.wait_send)
 
     def await_halo(source, target, turn):
         for copy in halo_copies(source, target, turn):
             copy.wait_recv()
 
+    send_halo(label, halo_label, 6)
     send_halo(rs, halo_rhs, 0)
+    for copy in loads[2:]:
+        copy.wait()
+
+    def greet_again(off, carry):
+        pl.semaphore_signal(
+            all_here, inc=1, device_id=(lax.rem(s + off, n_slab), c), device_id_type=MESH
+        )
+        return carry
+
+    lax.fori_loop(1, n_slab, greet_again, 0)
 
     blocks_f32[0:64, :] = vol_ref[...]
     blocks_f32[64:448, :] = side_ref[...]
@@ -207,70 +264,66 @@
         seen = seen + counted[:, LANES : 2 * LANES]
         rank_b[x, y] = jnp.broadcast_to(rank, (8, LANES))
 
-    def perm_of(label):
-        value = jnp.zeros_like(label)
+    def perm_of(kind):
+        value = jnp.zeros_like(kind)
         for k in range(16):
-            value = jnp.where(label == float(k), perm_ref[k], value)
+            value = jnp.where(kind == float(k), perm_ref[k], value)
         return value
 
     def own_perm(x, carry):
         for y in range(WIDE):
-            value = perm_of(rs[x, y, 64:72, :])
+            value = perm_of(label[x, y])
             perm_b[x, y] = value
             perm_inv[x, y] = 1.0 / value
         return carry
 
     lax.fori_loop(0, WIDE, own_perm, 0)
 
-    def slab_copy(turn, source, target, off, stage):
-        to = lax.rem(s + off, n_slab)
-        return pltpu.make_async_remote_copy(
-            src_ref=mail.at[turn, source, :, pl.ds(pl.multiple_of(to * n_cross, n_cross), n_cross)],
-            dst_ref=mail.at[turn, target, :, pl.ds(pl.multiple_of(s * n_cross, n_cross), n_cross)],
-            send_sem=mail_send.at[turn, stage],
-            recv_sem=mail_recv.at[turn, stage],
-            device_id=(to, c),
-            device_id_type=MESH,
-        )
-
-    def cross_copy(turn, source, target, off, stage):
-        to = lax.rem(c + off, n_cross)
-        return pltpu.make_async_remote_copy(
-            src_ref=mail.at[turn, source, :, pl.ds(pl.multiple_of(to * n_slab, n_slab), n_slab)],
-            dst_ref=mail.at[turn, target, :, pl.ds(pl.multiple_of(c * n_slab, n_slab), n_slab)],
-            send_sem=mail_send.at[turn, stage],
-            recv_sem=mail_recv.at[turn, stage],
-            device_id=(s, to),
-            device_id_type=MESH,
-        )
-
-    def post(turn, source, target, stage, along_slab):
-        def one(off, carry):
-            (slab_copy if along_slab else cross_copy)(turn, source, target, off, stage).start()
-            return carry
-
-        lax.fori_loop(1, n_slab if along_slab else n_cross, one, 0)
-        size, place = (n_cross, s) if along_slab else (n_slab, c)
-        rows = pl.ds(pl.multiple_of(place * size, size), size)
-        mail[turn, target, :, rows, :] = mail[turn, source, :, rows, :]
-
-    def rows_moved(along_slab):
-        return (n_slab - 1) * n_cross if along_slab else (n_cross - 1) * n_slab
-
-    def collect(turn, target, stage, along_slab):
-        part = mail.at[turn, target, :, pl.ds(0, rows_moved(along_slab))]
-        pltpu.make_async_copy(part, part, mail_recv.at[turn, stage]).wait()
-
-    def release(turn, source, stage, along_slab):
-        part = mail.at[turn, source, :, pl.ds(0, rows_moved(along_slab))]
-        pltpu.make_async_copy(part, part, mail_send.at[turn, stage]).wait()
+    side_y = WIDE
+    side_x = n_slab // side_y
+    me = s * n_cross + c
+    s_x, s_y = s // side_y, lax.rem(s, side_y)
+
+    def hops(step):
+        return min(step[0], side_x - step[0]) + min(step[1], side_y - step[1])
+
+    far_first = sorted(
+        ((i, j) for i in range(side_x) for j in range(side_y)), key=lambda step: -hops(step)
+    )
+
+    def post(turn):
+        for step in far_first:
+            to_slab = lax.rem(s_x + step[0], side_x) * side_y + lax.rem(s_y + step[1], side_y)
+
+            def one(off, carry):
+                to_cross = lax.rem(c + off, n_cross)
+                pltpu.make_async_remote_copy(
+                    src_ref=mail.at[turn, 0, to_slab * n_cross + to_cross],
+                    dst_ref=mail.at[turn, 1, me],
+                    send_sem=mail_send.at[turn],
+                    recv_sem=mail_recv.at[turn],
+                    device_id=(to_slab, to_cross),
+                    device_id_type=MESH,
+                ).start()
+                return carry
+
+            lax.fori_loop(0 if hops(step) else 1, n_cross, one, 0)
+        sent.append(functools.partial(release, turn))
+        mail[turn, 1, me] = mail[turn, 0, me]
+
+    def collect(turn):
+        part = mail.at[turn, 1, pl.ds(0, owners - 1)]
+        pltpu.make_async_copy(part, part, mail_recv.at[turn]).wait()
+
+    def release(turn):
+        part = mail.at[turn, 0, pl.ds(0, owners - 1)]
+        pltpu.make_async_copy(part, part, mail_send.at[turn]).wait()
 
     def write_mail(turn, value):
-        for h in range(cap // 16):
-            mail[turn, 0, h] = value[:, h * LANES : (h + 1) * LANES]
+        mail[turn, 0] = value.reshape(owners, cap // 16, LANES)
 
     def read_mail(turn):
-        return jnp.concatenate([mail[turn, 3, h].T for h in range(cap // 16)], axis=0)
+        return mail[turn, 1].reshape(owners, cap * 8).T
 
     def pack(load):
         def one(x, carry):
@@ -289,19 +342,10 @@
         pack(load)
         slots = dot_nt(owner_hot[0:owners, :], packed[...])
         write_mail(turn, slots[:, 0 : cap * 8] + slots[:, cap * 8 : 2 * cap * 8])
-        post(turn, 0, 1, 0, True)
-
-    def to_owner_middle(turn):
-        collect(turn, 1, 0, True)
-        for k in range(n_cross):
-            for h in range(cap // 16):
-                mail[turn, 2, h, k * n_slab : (k + 1) * n_slab, :] = mail[
-                    turn, 1, h, pl.ds(k, n_slab, stride=n_cross), :
-                ]
-        post(turn, 2, 3, 1, False)
+        post(turn)
 
     def to_owner_end(turn):
-        collect(turn, 3, 1, False)
+        collect(turn)
         return read_mail(turn)
 
     def gather_sum(arrived):
@@ -316,19 +360,10 @@
         flat = both[0:8] + both[8:16]
         out = jnp.concatenate([flat[:, owners * r : owners * (r + 1)] for r in range(cap)], axis=0)
         write_mail(turn, out.T)
-        post(turn, 0, 1, 0, False)
-
-    def from_owner_middle(turn):
-        collect(turn, 1, 0, False)
-        for k in range(n_slab):
-            for h in range(cap // 16):
-                mail[turn, 2, h, k * n_cross : (k + 1) * n_cross, :] = mail[
-                    turn, 1, h, pl.ds(k, n_cross, stride=n_slab), :
-                ]
-        post(turn, 2, 3, 1, True)
+        post(turn)
 
     def from_owner_end(turn, target):
-        collect(turn, 3, 1, True)
+        collect(turn)
         high, low = parts(read_mail(turn))
         spread = jnp.concatenate([high, low], axis=1).astype(BF16)
         for pair in range(WIDE * WIDE // 2):
@@ -416,13 +451,13 @@
         return results
 
     def label_of(x, y):
-        return rs[x, y, 64:72, :]
+        return label[x, y]
 
     def first_sweep(x, carry):
         for half in range(2):
             ys = (2 * half, 2 * half + 1)
             found = smoothed(
-                [rs[x, y, 0:64, :] for y in ys],
+                [rs[x, y] for y in ys],
                 [label_of(x, y) for y in ys],
                 [perm_inv[x, y] for y in ys],
             )
@@ -437,28 +472,14 @@
         label = jnp.broadcast_to(local_ref[pl.ds(x * WIDE + y, 1), :], (8, LANES)).astype(F32) + 1.0
         return jnp.where(row == 0, label, jnp.where(row == 1, perm_b[x, y], 0.0))
 
+    pl.semaphore_wait(all_here, n_slab - 1)
     to_owner_start(0, keys)
 
-    await_halo(rs, halo_rhs, 0)
+    await_halo(label, halo_label, 6)
     inside = (s > 0, s < n_slab - 1, c > 0, c < n_cross - 1)
-
-    def halo_sweep(side, carry):
-        label = [halo_rhs[side, j, 64:72, :] for j in range(WIDE)]
-        found = [perm_of(v) for v in label]
+    for side in range(4):
         for j in range(WIDE):
-            halo_coarse[0, side, j] = found[j]
-        for half in range(2):
-            js = (2 * half, 2 * half + 1)
-            values = smoothed(
-                [halo_rhs[side, j, 0:64, :] for j in js],
-                [label[j] for j in js],
-                [1.0 / found[j] for j in js],
-            )
-            for j, value in zip(js, values):
-                halos[3, side, j] = value
-        return carry
-
-    lax.fori_loop(0, 4, halo_sweep, 0)
+            halo_coarse[0, side, j] = perm_of(halo_label[side, j])
 
     for x in range(WIDE):
         for y in range(WIDE):
@@ -493,11 +514,27 @@
         return lambda x, y: stack_rows(ref[(*lead, x, y)])
 
     own_products(fine_stack(start_field), op_stack, 64)
+
+    await_halo(rs, halo_rhs, 0)
+
+    def halo_sweep(side, carry):
+        for half in range(2):
+            js = (2 * half, 2 * half + 1)
+            values = smoothed(
+                [halo_rhs[side, j] for j in js],
+                [halo_label[side, j] for j in js],
+                [1.0 / halo_coarse[0, side, j] for j in js],
+            )
+            for j, value in zip(js, values):
+                halos[3, side, j] = value
+        return carry
+
+    lax.fori_loop(0, 4, halo_sweep, 0)
     halo_products(fine_stack(halos, 3), op_stack, 64)
-    to_owner_middle(0)
-
-    def sweep(residue, iterate, target):
-        def one(x, carry):
+
+    def sweep(residue, iterate, target, turn):
+        def one(step, carry):
+            x = lax.rem(step * 3, WIDE)
             for half in range(2):
                 ys = (2 * half, 2 * half + 1)
                 found = smoothed(
@@ -507,14 +544,26 @@
                 )
                 for y, value in zip(ys, found):
                     fields[target, x, y] = iterate(x, y) + value
+
+            @pl.when(step == 0)
+            def _():
+                halo_copies(fields.at[target], halos.at[target], turn)[0].start()
+
+            @pl.when(step == 1)
+            def _():
+                halo_copies(fields.at[target], halos.at[target], turn)[1].start()
+
             return carry
 
         lax.fori_loop(0, WIDE, one, 0)
+        copies = halo_copies(fields.at[target], halos.at[target], turn)
+        copies[2].start()
+        copies[3].start()
+        sent.extend(copy.wait_send for copy in copies)
 
     sweep(
-        lambda x, y: rs[x, y, 0:64, :] - applied(x, y, 64), lambda x, y: start_field[x, y], 0
+        lambda x, y: rs[x, y] - applied(x, y, 64), lambda x, y: start_field[x, y], 0, 1
     )
-    send_halo(fields.at[0], halos.at[0], 1)
     own_products(fine_stack(fields, 0), op_stack, 64)
 
     arrived = to_owner_end(0)
@@ -532,7 +581,7 @@
     def second_residue(x, carry):
         rest = []
         for y in range(WIDE):
-            value = rs[x, y, 0:64, :] - applied(x, y, 64)
+            value = rs[x, y] - applied(x, y, 64)
             fine_res[x, y] = value
             rest.append(stack_rows(value))
         found = dot(restrict_cols, jnp.concatenate(rest, axis=1))
@@ -549,22 +598,18 @@
         return coarse_keep[0] * product
 
     to_owner_start(1, lambda x, y: coarse_field[2, x, y])
-    to_owner_middle(1)
     coarse_res = gather_sum(to_owner_end(1))
     first = coarse_step(coarse_res)
     from_owner_start(3, first)
-    from_owner_middle(3)
     from_owner_end(3, 0)
     send_halo(coarse_field.at[0], halo_coarse.at[1], 2)
     own_products(fine_stack(coarse_field, 0), coarse_stack, 8)
     await_halo(coarse_field.at[0], halo_coarse.at[1], 2)
     halo_products(fine_stack(halo_coarse, 1), coarse_stack, 8)
     to_owner_start(2, lambda x, y: applied(x, y, 8))
-    to_owner_middle(2)
     again = coarse_res - gather_sum(to_owner_end(2))
     second = first + coarse_step(again)
     from_owner_start(4, second)
-    from_owner_middle(4)
     from_owner_end(4, 1)
     send_halo(coarse_field.at[1], halo_coarse.at[2], 3)
 
@@ -574,39 +619,41 @@
     own_products(fine_stack(coarse_field, 1), prolong_stack, 64, add_prolonged)
     await_halo(coarse_field.at[1], halo_coarse.at[2], 3)
     halo_products(fine_stack(halo_coarse, 2), prolong_stack, 64)
-    sweep(lambda x, y: fine_res[x, y] - applied(x, y, 64), lambda x, y: start_field[x, y], 1)
-    send_halo(fields.at[1], halos.at[1], 4)
+    sweep(lambda x, y: fine_res[x, y] - applied(x, y, 64), lambda x, y: start_field[x, y], 1, 4)
 
     own_products(fine_stack(fields, 1), op_stack, 64)
     await_halo(fields.at[1], halos.at[1], 4)
     halo_products(fine_stack(halos, 1), op_stack, 64)
     sweep(
-        lambda x, y: rs[x, y, 0:64, :] - applied(x, y, 64), lambda x, y: fields[1, x, y], 2
+        lambda x, y: rs[x, y] - applied(x, y, 64), lambda x, y: fields[1, x, y], 2, 5
     )
-    send_halo(fields.at[2], halos.at[2], 5)
     own_products(fine_stack(fields, 2), op_stack, 64)
     for xy in range(WIDE * WIDE):
-        sol_ref[pl.ds(xy, 64, stride=WIDE * WIDE), :] = fields[2, xy // WIDE, xy % WIDE]
+        rhs_ref[pl.ds(xy, 64, stride=WIDE * WIDE), :] = fields[2, xy // WIDE, xy % WIDE]
+    store = pltpu.make_async_copy(rhs_ref, sol_ref, load_sem.at[0])
+    store.start()
     await_halo(fields.at[2], halos.at[2], 5)
     halo_products(fine_stack(halos, 2), op_stack, 64)
     for xy in range(WIDE * WIDE):
         x, y = xy // WIDE, xy % WIDE
-        res_ref[pl.ds(xy, 64, stride=WIDE * WIDE), :] = rs[x, y, 0:64, :] - applied(x, y, 64)
-
-    sent = (
-        (rs, halo_rhs, 0),
-        (fields.at[0], halos.at[0], 1),
-        (coarse_field.at[0], halo_coarse.at[1], 2),
-        (coarse_field.at[1], halo_coarse.at[2], 3),
-        (fields.at[1], halos.at[1], 4),
-        (fields.at[2], halos.at[2], 5),
-    )
-    for source, target, turn in sent:
-        for copy in halo_copies(source, target, turn):
-            copy.wait_send()
-    for turn in range(5):
-        release(turn, 0, 0, turn < 3)
-        release(turn, 2, 1, turn >= 3)
+        out_ref[pl.ds(xy, 64, stride=WIDE * WIDE), :] = rs[x, y] - applied(x, y, 64)
+
+    last = pltpu.make_async_copy(out_ref, res_ref, load_sem.at[1])
+    last.start()
+    drain()
+    store.wait()
+    last.wait()
+
+
+def hand_over(sol_in, res_in, sol_out, res_out, sem):
+    copies = [
+        pltpu.make_async_copy(sol_in, sol_out, sem.at[0]),
+        pltpu.make_async_copy(res_in, res_out, sem.at[1]),
+    ]
+    for copy in copies:
+        copy.start()
+    for copy in copies:
+        copy.wait()
 
 
 def local(
@@ -625,14 +672,27 @@
     owners,
     agg_local,
 ):
-    vmem = pl.BlockSpec(memory_space=pltpu.VMEM)
-    smem = pl.BlockSpec(memory_space=pltpu.SMEM)
+    anywhere = pl.BlockSpec(memory_space=pl.ANY)
     count = n_slab * n_cross
     face = (WIDE, WIDE)
     flat = jax.ShapeDtypeStruct((64 * WIDE * WIDE, LANES), F32)
     scratch = [
-        pltpu.VMEM((*face, 72, LANES), F32),
-        pltpu.VMEM((4, WIDE, 72, LANES), F32),
+        pltpu.VMEM((64 * WIDE * WIDE, LANES), F32),
+        pltpu.VMEM((WIDE * WIDE, LANES), jnp.int32),
+        pltpu.SMEM((16,), F32),
+        pltpu.VMEM((64, 64), F32),
+        pltpu.VMEM((6 * 64, 64), F32),
+        pltpu.VMEM((3 * 64, 64), F32),
+        pltpu.VMEM((16 * 64, 64), F32),
+        pltpu.VMEM((8, 64), F32),
+        pltpu.VMEM((8, 8), F32),
+        pltpu.VMEM((WIDE * WIDE, LANES), jnp.int32),
+        pltpu.VMEM((WIDE * WIDE, LANES), jnp.int32),
+        pltpu.VMEM((64 * WIDE * WIDE, LANES), F32),
+        pltpu.VMEM((*face, 64, LANES), F32),
+        pltpu.VMEM((4, WIDE, 64, LANES), F32),
+        pltpu.VMEM((*face, 8, LANES), F32),
+        pltpu.VMEM((4, WIDE, 8, LANES), F32),
         pltpu.VMEM((3, *face, 64, LANES), F32),
         pltpu.VMEM((4, 4, WIDE, 64, LANES), F32),
         pltpu.VMEM((*face, 64, LANES), F32),
@@ -654,24 +714,26 @@
         pltpu.VMEM((*face, 8, LANES), F32),
         pltpu.VMEM((2 * cap * 8, WIDE * WIDE * LANES), BF16),
         pltpu.VMEM((LANES, cap * count), BF16),
-        pltpu.VMEM((5, 4, cap // 16, count, LANES), F32),
+        pltpu.VMEM((5, 2, count, cap // 16, LANES), F32),
         pltpu.VMEM((1, 8, LANES), F32),
         pltpu.VMEM((3, *face, 8, LANES), F32),
         pltpu.VMEM((3, 4, WIDE, 8, LANES), F32),
-        pltpu.SemaphoreType.DMA((6, 4)),
-        pltpu.SemaphoreType.DMA((6, 4)),
-        pltpu.SemaphoreType.DMA((5, 2)),
-        pltpu.SemaphoreType.DMA((5, 2)),
+        pltpu.SemaphoreType.DMA((11,)),
+        pltpu.SemaphoreType.DMA((7, 4)),
+        pltpu.SemaphoreType.DMA((7, 4)),
+        pltpu.SemaphoreType.DMA((5,)),
+        pltpu.SemaphoreType.DMA((5,)),
+        pltpu.SemaphoreType.REGULAR,
     ]
     flops = 2 * 2048 * (5 * 832 + 5 * 1024) * 192
     solved, residue = pl.pallas_call(
         functools.partial(cycle, n_slab, n_cross, cap),
         out_shape=(flat, flat),
-        in_specs=[vmem, vmem, smem] + [vmem] * 8,
-        out_specs=(vmem, vmem),
+        in_specs=[pl.BlockSpec(memory_space=pltpu.HBM)] * 11,
+        out_specs=(anywhere, anywhere),
         scratch_shapes=scratch,
         compiler_params=pltpu.CompilerParams(
-            collective_id=0, has_side_effects=True, vmem_limit_bytes=56 * 1024 * 1024
+            collective_id=0, has_side_effects=True, vmem_limit_bytes=62 * 1024 * 1024
         ),
         cost_estimate=pl.CostEstimate(flops=flops, bytes_accessed=4 << 20, transcendentals=0),
     )(
@@ -687,6 +749,14 @@
         owners.reshape(WIDE * WIDE, LANES),
         agg_local.reshape(WIDE * WIDE, LANES),
     )
+    solved, residue = pl.pallas_call(
+        hand_over,
+        out_shape=(flat, flat),
+        in_specs=[anywhere] * 2,
+        out_specs=(anywhere, anywhere),
+        scratch_shapes=[pltpu.SemaphoreType.DMA((2,))],
+        compiler_params=pltpu.CompilerParams(vmem_limit_bytes=62 * 1024 * 1024),
+    )(solved, residue)
     return solved.reshape(rhs.shape), residue.reshape(rhs.shape)
 
 

time: 102 us -> 118 us (1.16)
  Pallas kernels: 98.5 us -> 117 us
  local copies, waits for them, and re-layouts: 2.72 us -> 0 us
    pallas_call x0 -> x1, Pallas kernels: none -> 32.9 us  [local(): pl.pallas_call(hand_over, out_shape=(flat, flat), in_specs=[anywhere] * 2...]
    pallas_call x1, Pallas kernels: 98.5 us -> 83.7 us  [local(): pl.pallas_call(functools.partial(cycle, n_slab, n_cross, cap), out_shape=...]
    unnamed x4 -> x0, local copies, waits for them, and re-layouts: 2.72 us -> none
where the time goes in v2:
time: 118 us; the launch traced here: 117 us
  Pallas kernels  117 us (99%)
    pallas_call x1, Pallas kernels, local(): pl.pallas_call(functools.partial(cycle, n_slab, n_cross, cap), out_shape=...  83.7 us
    pallas_call x1, Pallas kernels, local(): pl.pallas_call(hand_over, out_shape=(flat, flat), in_specs=[anywhere] * 2...  32.9 us

profile of v2, /device:TPU:0, one launch (start us, length us, event | category | flops | bytes accessed | tf_op | source)
XLA Modules:
  0.0 117.2 jit_solution(8305294304954458975)
XLA Ops:
  0.6 83.7 %shard_map.122 = (f32[1024,128]{1,0:T(8,128)}, f32[1024,128]{1,0:T(8,128)}) custom-call(f32[1024,128]{1,0:T(8,128)} %bitcast.9, s32[16,128]{1,0:T(8,128)} %bitcast.15, f32[16]{0:T(128)} %perm_hbm.1, f32[64,64]{1,0:T(8,128)} %vol_hbm.1, f32[384,64]{1,0:T(8,128)} %bitcast.13, f32[192,64]{1,0:T(8,128)} %bitcast.14, f32[1024,64]{1,0:T(8,128)} %bitcast.10, ...), custom_call_target="tpu_custom_call" | custom-call | flops 7298088960 | bytes 4194304 | tf_op jit(solution)/shard_map/pallas_call | solution.py:729
  84.3 32.9 %shard_map.123 = (f32[1024,128]{1,0:T(8,128)}, f32[1024,128]{1,0:T(8,128)}) custom-call(f32[1024,128]{1,0:T(8,128)} %get-tuple-element.6.sol_in, f32[1024,128]{1,0:T(8,128)} %get-tuple-element.7.res_in), custom_call_target="tpu_custom_call" | custom-call | tf_op jit(solution)/shard_map/pallas_call | solution.py:752

commit v3 on v2

--- a/solution.py
+++ b/solution.py
@@ -73,7 +73,6 @@
     coarse_ref,
     owner_ref,
     local_ref,
-    out_ref,
     rs,
     halo_rhs,
     label,
@@ -629,20 +628,14 @@
     )
     own_products(fine_stack(fields, 2), op_stack, 64)
     for xy in range(WIDE * WIDE):
-        rhs_ref[pl.ds(xy, 64, stride=WIDE * WIDE), :] = fields[2, xy // WIDE, xy % WIDE]
-    store = pltpu.make_async_copy(rhs_ref, sol_ref, load_sem.at[0])
-    store.start()
+        sol_ref[pl.ds(xy, 64, stride=WIDE * WIDE), :] = fields[2, xy // WIDE, xy % WIDE]
     await_halo(fields.at[2], halos.at[2], 5)
     halo_products(fine_stack(halos, 2), op_stack, 64)
     for xy in range(WIDE * WIDE):
         x, y = xy // WIDE, xy % WIDE
-        out_ref[pl.ds(xy, 64, stride=WIDE * WIDE), :] = rs[x, y] - applied(x, y, 64)
-
-    last = pltpu.make_async_copy(out_ref, res_ref, load_sem.at[1])
-    last.start()
+        res_ref[pl.ds(xy, 64, stride=WIDE * WIDE), :] = rs[x, y] - applied(x, y, 64)
+
     drain()
-    store.wait()
-    last.wait()
 
 
 def hand_over(sol_in, res_in, sol_out, res_out, sem):
@@ -688,7 +681,6 @@
         pltpu.VMEM((8, 8), F32),
         pltpu.VMEM((WIDE * WIDE, LANES), jnp.int32),
         pltpu.VMEM((WIDE * WIDE, LANES), jnp.int32),
-        pltpu.VMEM((64 * WIDE * WIDE, LANES), F32),
         pltpu.VMEM((*face, 64, LANES), F32),
         pltpu.VMEM((4, WIDE, 64, LANES), F32),
         pltpu.VMEM((*face, 8, LANES), F32),
@@ -726,17 +718,9 @@
         pltpu.SemaphoreType.REGULAR,
     ]
     flops = 2 * 2048 * (5 * 832 + 5 * 1024) * 192
-    solved, residue = pl.pallas_call(
-        functools.partial(cycle, n_slab, n_cross, cap),
-        out_shape=(flat, flat),
-        in_specs=[pl.BlockSpec(memory_space=pltpu.HBM)] * 11,
-        out_specs=(anywhere, anywhere),
-        scratch_shapes=scratch,
-        compiler_params=pltpu.CompilerParams(
-            collective_id=0, has_side_effects=True, vmem_limit_bytes=62 * 1024 * 1024
-        ),
-        cost_estimate=pl.CostEstimate(flops=flops, bytes_accessed=4 << 20, transcendentals=0),
-    )(
+    kept = pltpu.VMEM(flat.shape, F32)
+    vmem = pl.BlockSpec(memory_space=pltpu.VMEM)
+    arguments = (
         rhs.reshape(64 * WIDE * WIDE, LANES),
         classes.reshape(WIDE * WIDE, LANES),
         perm,
@@ -750,12 +734,22 @@
         agg_local.reshape(WIDE * WIDE, LANES),
     )
     solved, residue = pl.pallas_call(
+        functools.partial(cycle, n_slab, n_cross, cap),
+        out_shape=(kept, kept),
+        in_specs=[pl.BlockSpec(memory_space=pltpu.HBM)] * 11,
+        out_specs=(vmem, vmem),
+        scratch_shapes=scratch,
+        compiler_params=pltpu.CompilerParams(
+            collective_id=0, has_side_effects=True, vmem_limit_bytes=40 * 1024 * 1024
+        ),
+        cost_estimate=pl.CostEstimate(flops=flops, bytes_accessed=4 << 20, transcendentals=0),
+    )(*(pltpu.with_memory_space_constraint(value, pltpu.HBM) for value in arguments))
+    solved, residue = pl.pallas_call(
         hand_over,
         out_shape=(flat, flat),
-        in_specs=[anywhere] * 2,
+        in_specs=[vmem, vmem],
         out_specs=(anywhere, anywhere),
         scratch_shapes=[pltpu.SemaphoreType.DMA((2,))],
-        compiler_params=pltpu.CompilerParams(vmem_limit_bytes=62 * 1024 * 1024),
     )(solved, residue)
     return solved.reshape(rhs.shape), residue.reshape(rhs.shape)
 

time: 118 us -> 87.7 us (0.74)
  Pallas kernels: 117 us -> 85.1 us
  local copies, waits for them, and re-layouts: 0 us -> 1.56 us
    pallas_call x1, Pallas kernels: 32.9 us -> 2.18 us  [local(): pl.pallas_call(hand_over, out_shape=(flat, flat), in_specs=[vmem, vmem],...]
    unnamed x0 -> x4, local copies, waits for them, and re-layouts: none -> 1.56 us
where the time goes in v3:
time: 87.7 us; the launch traced here: 87.3 us
  Pallas kernels  85.1 us (97%)
  local copies, waits for them, and re-layouts  1.56 us (2%)
    pallas_call x1, Pallas kernels, local(): pl.pallas_call(functools.partial(cycle, n_slab, n_cross, cap), out_shape=...  82.9 us
    pallas_call x1, Pallas kernels, local(): pl.pallas_call(hand_over, out_shape=(flat, flat), in_specs=[vmem, vmem],...  2.18 us

profile of v3, /device:TPU:0, one launch (start us, length us, event | category | flops | bytes accessed | tf_op | source)
XLA Modules:
  0.0 87.3 jit_solution(5132739376776537505)
XLA Ops:
  0.6 82.9 %shard_map.122 = (f32[1024,128]{1,0:T(8,128)S(1)}, f32[1024,128]{1,0:T(8,128)S(1)}) custom-call(f32[1024,128]{1,0:T(8,128)} %bitcast.9, s32[16,128]{1,0:T(8,128)} %bitcast.15, f32[16]{0:T(128)} %perm_hbm.1, f32[64,64]{1,0:T(8,128)} %vol_hbm.1, f32[384,64]{1,0:T(8,128)} %bitcast.13, f32[192,64]{1,0:T(8,128)} %bitcast.14, f32[1024,64]{1,0:T(8,128)} %bitcast.10, ...), custom_call_target="tpu_custom_call" | custom-call | flops 7298088960 | bytes 4194304 | tf_op jit(solution)/shard_map/pallas_call | solution.py:736
  83.6 0.0 copy-start
  83.6 0.8 copy-done
  84.4 0.0 copy-start.1
  84.4 0.8 copy-done.1
  85.2 2.2 %shard_map.123 = (f32[1024,128]{1,0:T(8,128)}, f32[1024,128]{1,0:T(8,128)}) custom-call(f32[1024,128]{1,0:T(8,128)} %copy-done, f32[1024,128]{1,0:T(8,128)} %copy-done.1), custom_call_target="tpu_custom_call" | custom-call | tf_op jit(solution)/shard_map/pallas_call | solution.py:747
Async XLA Ops:
  83.6 0.8 copy-start
  84.4 0.8 copy-start.1

commit v4 on v3

--- a/solution.py
+++ b/solution.py
@@ -74,7 +74,6 @@
     owner_ref,
     local_ref,
     rs,
-    halo_rhs,
     label,
     halo_label,
     fields,
@@ -152,15 +151,13 @@
     ]
     for copy in loads:
         copy.start()
-    loads[0].wait()
-    loads[1].wait()
+    for k in (0, 1, 2, 6):
+        loads[k].wait()
 
     for xy in range(WIDE * WIDE):
         x, y = xy // WIDE, xy % WIDE
         rs[x, y] = rhs_ref[pl.ds(xy, 64, stride=WIDE * WIDE), :]
         label[x, y] = jnp.broadcast_to(class_ref[xy : xy + 1, :], (8, LANES)).astype(F32)
-
-    pl.semaphore_wait(barrier, n_slab + n_cross - 2)
 
     sent = []
 
@@ -196,10 +193,65 @@
         for copy in halo_copies(source, target, turn):
             copy.wait_recv()
 
+    def perm_of(kind):
+        value = jnp.zeros_like(kind)
+        for k in range(16):
+            value = jnp.where(kind == float(k), perm_ref[k], value)
+        return value
+
+    def own_perm(x, carry):
+        for y in range(WIDE):
+            value = perm_of(label[x, y])
+            perm_b[x, y] = value
+            perm_inv[x, y] = 1.0 / value
+        return carry
+
+    lax.fori_loop(0, WIDE, own_perm, 0)
+
+    for m in range(16):
+        rows = slice(64 * m, 64 * m + 64)
+        smooth_stack[rows, :] = stack_columns(smooth_ref[rows, :])
+
+    def smoothed(values, labels, inverses):
+        product = dot(smooth_stack[...], jnp.concatenate([stack_rows(v) for v in values], axis=1))
+        results = []
+        for i, (label, inverse) in enumerate(zip(labels, inverses)):
+            columns = slice(i * LANES, (i + 1) * LANES)
+            value = product[0:64, columns].reshape(8, 8, LANES)
+            for k in range(1, 16):
+                block = product[64 * k : 64 * k + 64, columns].reshape(8, 8, LANES)
+                value = jnp.where((label == float(k))[None], block, value)
+            results.append((value * inverse[None]).reshape(64, LANES))
+        return results
+
+    def label_of(x, y):
+        return label[x, y]
+
+    def first_sweep(step, carry):
+        x = lax.rem(step * 3, WIDE)
+        for half in range(2):
+            ys = (2 * half, 2 * half + 1)
+            found = smoothed(
+                [rs[x, y] for y in ys],
+                [label_of(x, y) for y in ys],
+                [perm_inv[x, y] for y in ys],
+            )
+            for y, value in zip(ys, found):
+                start_field[x, y] = value
+        return carry
+
+    lax.fori_loop(0, 2, first_sweep, 0)
+    pl.semaphore_wait(barrier, n_slab + n_cross - 2)
     send_halo(label, halo_label, 6)
-    send_halo(rs, halo_rhs, 0)
-    for copy in loads[2:]:
-        copy.wait()
+    first_copies = halo_copies(start_field, halos.at[3], 0)
+    first_copies[0].start()
+    first_copies[1].start()
+    lax.fori_loop(2, WIDE, first_sweep, 0)
+    first_copies[2].start()
+    first_copies[3].start()
+    sent.extend(copy.wait_send for copy in first_copies)
+    for k in (3, 4, 5, 7, 8, 9, 10):
+        loads[k].wait()
 
     def greet_again(off, carry):
         pl.semaphore_signal(
@@ -223,9 +275,6 @@
     for m in range(13):
         rows = slice(64 * m, 64 * m + 64)
         op_stack[rows, :] = stack_columns(blocks_f32[rows, :])
-    for m in range(16):
-        rows = slice(64 * m, 64 * m + 64)
-        smooth_stack[rows, :] = stack_columns(smooth_ref[rows, :])
     restrict = restrict_ref[...]
     short = lax.dot_general(
         blocks_f32[...], restrict, NT, precision=HIGHEST, preferred_element_type=F32
@@ -263,21 +312,6 @@
         seen = seen + counted[:, LANES : 2 * LANES]
         rank_b[x, y] = jnp.broadcast_to(rank, (8, LANES))
 
-    def perm_of(kind):
-        value = jnp.zeros_like(kind)
-        for k in range(16):
-            value = jnp.where(kind == float(k), perm_ref[k], value)
-        return value
-
-    def own_perm(x, carry):
-        for y in range(WIDE):
-            value = perm_of(label[x, y])
-            perm_b[x, y] = value
-            perm_inv[x, y] = 1.0 / value
-        return carry
-
-    lax.fori_loop(0, WIDE, own_perm, 0)
-
     side_y = WIDE
     side_x = n_slab // side_y
     me = s * n_cross + c
@@ -306,7 +340,7 @@
                 ).start()
                 return carry
 
-            lax.fori_loop(0 if hops(step) else 1, n_cross, one, 0)
+            lax.fori_loop(0 if hops(step) else 1, n_cross, one, 0, unroll=True)
         sent.append(functools.partial(release, turn))
         mail[turn, 1, me] = mail[turn, 0, me]
 
@@ -436,43 +470,6 @@
         total = total - scaled(weights[8, x, y], gy0[x, y, 0:rows, :])
         total = total - scaled(weights[9, x, y], gy1[x, y + 1, 0:rows, :])
         return total.reshape(rows, LANES)
-
-    def smoothed(values, labels, inverses):
-        product = dot(smooth_stack[...], jnp.concatenate([stack_rows(v) for v in values], axis=1))
-        results = []
-        for i, (label, inverse) in enumerate(zip(labels, inverses)):
-            columns = slice(i * LANES, (i + 1) * LANES)
-            value = product[0:64, columns].reshape(8, 8, LANES)
-            for k in range(1, 16):
-                block = product[64 * k : 64 * k + 64, columns].reshape(8, 8, LANES)
-                value = jnp.where((label == float(k))[None], block, value)
-            results.append((value * inverse[None]).reshape(64, LANES))
-        return results
-
-    def label_of(x, y):
-        return label[x, y]
-
-    def first_sweep(x, carry):
-        for half in range(2):
-            ys = (2 * half, 2 * half + 1)
-            found = smoothed(
-                [rs[x, y] for y in ys],
-                [label_of(x, y) for y in ys],
-                [perm_inv[x, y] for y in ys],
-            )
-            for y, value in zip(ys, found):
-                start_field[x, y] = value
-        return carry
-
-    lax.fori_loop(0, WIDE, first_sweep, 0)
-
-    def keys(x, y):
-        row = lax.broadcasted_iota(jnp.int32, (8, LANES), 0)
-        label = jnp.broadcast_to(local_ref[pl.ds(x * WIDE + y, 1), :], (8, LANES)).astype(F32) + 1.0
-        return jnp.where(row == 0, label, jnp.where(row == 1, perm_b[x, y], 0.0))
-
-    pl.semaphore_wait(all_here, n_slab - 1)
-    to_owner_start(0, keys)
 
     await_halo(label, halo_label, 6)
     inside = (s > 0, s < n_slab - 1, c > 0, c < n_cross - 1)
@@ -514,21 +511,7 @@
 
     own_products(fine_stack(start_field), op_stack, 64)
 
-    await_halo(rs, halo_rhs, 0)
-
-    def halo_sweep(side, carry):
-        for half in range(2):
-            js = (2 * half, 2 * half + 1)
-            values = smoothed(
-                [halo_rhs[side, j] for j in js],
-                [halo_label[side, j] for j in js],
-                [1.0 / halo_coarse[0, side, j] for j in js],
-            )
-            for j, value in zip(js, values):
-                halos[3, side, j] = value
-        return carry
-
-    lax.fori_loop(0, 4, halo_sweep, 0)
+    await_halo(start_field, halos.at[3], 0)
     halo_products(fine_stack(halos, 3), op_stack, 64)
 
     def sweep(residue, iterate, target, turn):
@@ -565,14 +548,13 @@
     )
     own_products(fine_stack(fields, 0), op_stack, 64)
 
-    arrived = to_owner_end(0)
-    hot_ids = lax.broadcasted_iota(jnp.int32, (LANES, owners), 0).astype(F32) + 1.0
-    for r in range(cap):
-        local_hot[:, r * owners : (r + 1) * owners] = jnp.where(
-            hot_ids == arrived[8 * r : 8 * r + 1, :], 1.0, 0.0
-        ).astype(BF16)
-    perm_sum = gather_sum(arrived)[1:2, :]
-    coarse_keep[0] = jnp.broadcast_to(1.0 / (1.0 + perm_sum), (8, LANES))
+    def keys(x, y):
+        row = lax.broadcasted_iota(jnp.int32, (8, LANES), 0)
+        label = jnp.broadcast_to(local_ref[pl.ds(x * WIDE + y, 1), :], (8, LANES)).astype(F32) + 1.0
+        return jnp.where(row == 0, label, jnp.where(row == 1, perm_b[x, y], 0.0))
+
+    pl.semaphore_wait(all_here, n_slab - 1)
+    to_owner_start(0, keys)
 
     await_halo(fields.at[0], halos.at[0], 1)
     halo_products(fine_stack(halos, 0), op_stack, 64)
@@ -597,6 +579,15 @@
         return coarse_keep[0] * product
 
     to_owner_start(1, lambda x, y: coarse_field[2, x, y])
+    arrived = to_owner_end(0)
+    hot_ids = lax.broadcasted_iota(jnp.int32, (LANES, owners), 0).astype(F32) + 1.0
+    for r in range(cap):
+        local_hot[:, r * owners : (r + 1) * owners] = jnp.where(
+            hot_ids == arrived[8 * r : 8 * r + 1, :], 1.0, 0.0
+        ).astype(BF16)
+    perm_sum = gather_sum(arrived)[1:2, :]
+    coarse_keep[0] = jnp.broadcast_to(1.0 / (1.0 + perm_sum), (8, LANES))
+
     coarse_res = gather_sum(to_owner_end(1))
     first = coarse_step(coarse_res)
     from_owner_start(3, first)
@@ -613,12 +604,12 @@
     send_halo(coarse_field.at[1], halo_coarse.at[2], 3)
 
     def add_prolonged(x, y, value):
-        start_field[x, y] = fields[0, x, y] + value
+        fields[3, x, y] = fields[0, x, y] + value
 
     own_products(fine_stack(coarse_field, 1), prolong_stack, 64, add_prolonged)
     await_halo(coarse_field.at[1], halo_coarse.at[2], 3)
     halo_products(fine_stack(halo_coarse, 2), prolong_stack, 64)
-    sweep(lambda x, y: fine_res[x, y] - applied(x, y, 64), lambda x, y: start_field[x, y], 1, 4)
+    sweep(lambda x, y: fine_res[x, y] - applied(x, y, 64), lambda x, y: fields[3, x, y], 1, 4)
 
     own_products(fine_stack(fields, 1), op_stack, 64)
     await_halo(fields.at[1], halos.at[1], 4)
@@ -639,9 +630,13 @@
 
 
 def hand_over(sol_in, res_in, sol_out, res_out, sem):
+    rows = sol_in.shape[0] // 4
     copies = [
-        pltpu.make_async_copy(sol_in, sol_out, sem.at[0]),
-        pltpu.make_async_copy(res_in, res_out, sem.at[1]),
+        pltpu.make_async_copy(
+            source.at[pl.ds(k * rows, rows)], target.at[pl.ds(k * rows, rows)], sem.at[i, k]
+        )
+        for i, (source, target) in enumerate(((sol_in, sol_out), (res_in, res_out)))
+        for k in range(4)
     ]
     for copy in copies:
         copy.start()
@@ -665,7 +660,6 @@
     owners,
     agg_local,
 ):
-    anywhere = pl.BlockSpec(memory_space=pl.ANY)
     count = n_slab * n_cross
     face = (WIDE, WIDE)
     flat = jax.ShapeDtypeStruct((64 * WIDE * WIDE, LANES), F32)
@@ -682,10 +676,9 @@
         pltpu.VMEM((WIDE * WIDE, LANES), jnp.int32),
         pltpu.VMEM((WIDE * WIDE, LANES), jnp.int32),
         pltpu.VMEM((*face, 64, LANES), F32),
-        pltpu.VMEM((4, WIDE, 64, LANES), F32),
         pltpu.VMEM((*face, 8, LANES), F32),
         pltpu.VMEM((4, WIDE, 8, LANES), F32),
-        pltpu.VMEM((3, *face, 64, LANES), F32),
+        pltpu.VMEM((4, *face, 64, LANES), F32),
         pltpu.VMEM((4, 4, WIDE, 64, LANES), F32),
         pltpu.VMEM((*face, 64, LANES), F32),
         pltpu.VMEM((*face, 64, LANES), F32),
@@ -746,10 +739,10 @@
     )(*(pltpu.with_memory_space_constraint(value, pltpu.HBM) for value in arguments))
     solved, residue = pl.pallas_call(
         hand_over,
-        out_shape=(flat, flat),
+        out_shape=(pltpu.HBM(flat.shape, F32),) * 2,
         in_specs=[vmem, vmem],
-        out_specs=(anywhere, anywhere),
-        scratch_shapes=[pltpu.SemaphoreType.DMA((2,))],
+        out_specs=(pl.BlockSpec(memory_space=pltpu.HBM),) * 2,
+        scratch_shapes=[pltpu.SemaphoreType.DMA((2, 4))],
     )(solved, residue)
     return solved.reshape(rhs.shape), residue.reshape(rhs.shape)
 

time: 87.7 us -> 82.6 us (0.942)
  Pallas kernels: 85.1 us -> 80 us
    pallas_call x1, Pallas kernels: 82.9 us -> 77.8 us  [local(): pl.pallas_call(functools.partial(cycle, n_slab, n_cross, cap), out_shape=...]
where the time goes in v4:
time: 82.6 us; the launch traced here: 82.4 us
  Pallas kernels  80 us (97%)
  local copies, waits for them, and re-layouts  1.56 us (2%)
    pallas_call x1, Pallas kernels, local(): pl.pallas_call(functools.partial(cycle, n_slab, n_cross, cap), out_shape=...  77.8 us
    pallas_call x1, Pallas kernels, local(): pl.pallas_call(hand_over, out_shape=(pltpu.HBM(flat.shape, F32),) * 2, in...  2.22 us

profile of v4, /device:TPU:0, one launch (start us, length us, event | category | flops | bytes accessed | tf_op | source)
XLA Modules:
  0.0 82.4 jit_solution(149063992357443930)
XLA Ops:
  0.6 77.8 %shard_map.122 = (f32[1024,128]{1,0:T(8,128)S(1)}, f32[1024,128]{1,0:T(8,128)S(1)}) custom-call(f32[1024,128]{1,0:T(8,128)} %bitcast.9, s32[16,128]{1,0:T(8,128)} %bitcast.15, f32[16]{0:T(128)} %perm_hbm.1, f32[64,64]{1,0:T(8,128)} %vol_hbm.1, f32[384,64]{1,0:T(8,128)} %bitcast.13, f32[192,64]{1,0:T(8,128)} %bitcast.14, f32[1024,64]{1,0:T(8,128)} %bitcast.10, ...), custom_call_target="tpu_custom_call" | custom-call | flops 7298088960 | bytes 4194304 | tf_op jit(solution)/shard_map/pallas_call | solution.py:729
  78.4 0.0 copy-start
  78.5 0.8 copy-done
  79.2 0.0 copy-start.1
  79.2 0.8 copy-done.1
  80.0 2.2 %shard_map.123 = (f32[1024,128]{1,0:T(8,128)}, f32[1024,128]{1,0:T(8,128)}) custom-call(f32[1024,128]{1,0:T(8,128)} %copy-done, f32[1024,128]{1,0:T(8,128)} %copy-done.1), custom_call_target="tpu_custom_call" | custom-call | tf_op jit(solution)/shard_map/pallas_call | solution.py:740
Async XLA Ops:
  78.4 0.8 copy-start
  79.2 0.8 copy-start.1

commit v5 on v4

--- a/solution.py
+++ b/solution.py
@@ -149,10 +149,12 @@
             )
         )
     ]
-    for copy in loads:
-        copy.start()
+    for k in (0, 1, 2, 6):
+        loads[k].start()
     for k in (0, 1, 2, 6):
         loads[k].wait()
+    for k in (3, 4, 5, 7, 8, 9, 10):
+        loads[k].start()
 
     for xy in range(WIDE * WIDE):
         x, y = xy // WIDE, xy % WIDE
@@ -228,7 +230,7 @@
         return label[x, y]
 
     def first_sweep(step, carry):
-        x = lax.rem(step * 3, WIDE)
+        x = step * 3 % WIDE
         for half in range(2):
             ys = (2 * half, 2 * half + 1)
             found = smoothed(
@@ -240,13 +242,15 @@
                 start_field[x, y] = value
         return carry
 
-    lax.fori_loop(0, 2, first_sweep, 0)
+    first_sweep(0, 0)
+    first_sweep(1, 0)
     pl.semaphore_wait(barrier, n_slab + n_cross - 2)
     send_halo(label, halo_label, 6)
     first_copies = halo_copies(start_field, halos.at[3], 0)
     first_copies[0].start()
     first_copies[1].start()
-    lax.fori_loop(2, WIDE, first_sweep, 0)
+    first_sweep(2, 0)
+    first_sweep(3, 0)
     first_copies[2].start()
     first_copies[3].start()
     sent.extend(copy.wait_send for copy in first_copies)
@@ -369,7 +373,8 @@
                     packed[i * cap * 8 : (i + 1) * cap * 8, columns] = spread.astype(BF16)
             return carry
 
-        lax.fori_loop(0, WIDE, one, 0)
+        for x in range(WIDE):
+            one(x, 0)
 
     def to_owner_start(turn, load):
         pack(load)
@@ -440,7 +445,8 @@
                         extra(x, y, block(13))
             return carry
 
-        lax.fori_loop(0, WIDE, one, 0)
+        for x in range(WIDE):
+            one(x, 0)
 
     def halo_products(load, stack, rows):
         for side in range(4):
@@ -515,8 +521,8 @@
     halo_products(fine_stack(halos, 3), op_stack, 64)
 
     def sweep(residue, iterate, target, turn):
-        def one(step, carry):
-            x = lax.rem(step * 3, WIDE)
+        copies = halo_copies(fields.at[target], halos.at[target], turn)
+        for step, x in enumerate((0, WIDE - 1, 1, 2)):
             for half in range(2):
                 ys = (2 * half, 2 * half + 1)
                 found = smoothed(
@@ -526,19 +532,8 @@
                 )
                 for y, value in zip(ys, found):
                     fields[target, x, y] = iterate(x, y) + value
-
-            @pl.when(step == 0)
-            def _():
-                halo_copies(fields.at[target], halos.at[target], turn)[0].start()
-
-            @pl.when(step == 1)
-            def _():
-                halo_copies(fields.at[target], halos.at[target], turn)[1].start()
-
-            return carry
-
-        lax.fori_loop(0, WIDE, one, 0)
-        copies = halo_copies(fields.at[target], halos.at[target], turn)
+            if step < 2:
+                copies[step].start()
         copies[2].start()
         copies[3].start()
         sent.extend(copy.wait_send for copy in copies)
@@ -570,7 +565,8 @@
             coarse_field[2, x, y] = found[0:8, y * LANES : (y + 1) * LANES]
         return carry
 
-    lax.fori_loop(0, WIDE, second_residue, 0)
+    for x in range(WIDE):
+        second_residue(x, 0)
 
     def coarse_step(value):
         product = jnp.dot(
@@ -743,7 +739,8 @@
         in_specs=[vmem, vmem],
         out_specs=(pl.BlockSpec(memory_space=pltpu.HBM),) * 2,
         scratch_shapes=[pltpu.SemaphoreType.DMA((2, 4))],
-    )(solved, residue)
+        compiler_params=pltpu.CompilerParams(vmem_limit_bytes=8 * 1024 * 1024),
+    )(*(pltpu.with_memory_space_constraint(value, pltpu.VMEM) for value in (solved, residue)))
     return solved.reshape(rhs.shape), residue.reshape(rhs.shape)
 
 

time: 82.6 us -> 78.1 us (0.946)
  Pallas kernels: 80 us -> 77.1 us
  local copies, waits for them, and re-layouts: 1.56 us -> 0 us
    pallas_call x1, Pallas kernels: 77.8 us -> 76.1 us  [local(): pl.pallas_call(functools.partial(cycle, n_slab, n_cross, cap), out_shape=...]
    unnamed x4 -> x0, local copies, waits for them, and re-layouts: 1.56 us -> none
    pallas_call x1, Pallas kernels: 2.22 us -> 1.03 us  [local(): pl.pallas_call(hand_over, out_shape=(pltpu.HBM(flat.shape, F32),) * 2, in...]
where the time goes in v5:
time: 78.1 us; the launch traced here: 77.9 us
  Pallas kernels  77.1 us (99%)
  between operations  0.8 us (1%)
    pallas_call x1, Pallas kernels, local(): pl.pallas_call(functools.partial(cycle, n_slab, n_cross, cap), out_shape=...  76.1 us

profile of v5, /device:TPU:0, one launch (start us, length us, event | category | flops | bytes accessed | tf_op | source)
XLA Modules:
  0.0 77.9 jit_solution(2374334479624652733)
XLA Ops:
  0.6 76.1 %shard_map.122 = (f32[1024,128]{1,0:T(8,128)S(1)}, f32[1024,128]{1,0:T(8,128)S(1)}) custom-call(f32[1024,128]{1,0:T(8,128)} %bitcast.9, s32[16,128]{1,0:T(8,128)} %bitcast.15, f32[16]{0:T(128)} %perm_hbm.1, f32[64,64]{1,0:T(8,128)} %vol_hbm.1, f32[384,64]{1,0:T(8,128)} %bitcast.13, f32[192,64]{1,0:T(8,128)} %bitcast.14, f32[1024,64]{1,0:T(8,128)} %bitcast.10, ...), custom_call_target="tpu_custom_call" | custom-call | flops 7298088960 | bytes 4194304 | tf_op jit(solution)/shard_map/pallas_call | solution.py:725
  76.7 1.0 %shard_map.123 = (f32[1024,128]{1,0:T(8,128)}, f32[1024,128]{1,0:T(8,128)}) custom-call(f32[1024,128]{1,0:T(8,128)S(1)} %get-tuple-element.6.sol_in, f32[1024,128]{1,0:T(8,128)S(1)} %get-tuple-element.7.res_in), custom_call_target="tpu_custom_call" | custom-call | tf_op jit(solution)/shard_map/pallas_call | solution.py:736

commit v6 on v5

--- a/solution.py
+++ b/solution.py
@@ -114,23 +114,6 @@
     c_up, c_down = lax.rem(c + 1, n_cross), lax.rem(c + n_cross - 1, n_cross)
     lane = lax.broadcasted_iota(jnp.int32, (8, LANES), 1)
 
-    barrier = pltpu.get_barrier_semaphore()
-
-    def greet_slab(off, carry):
-        pl.semaphore_signal(
-            barrier, inc=1, device_id=(lax.rem(s + off, n_slab), c), device_id_type=MESH
-        )
-        return carry
-
-    def greet_cross(off, carry):
-        pl.semaphore_signal(
-            barrier, inc=1, device_id=(s, lax.rem(c + off, n_cross)), device_id_type=MESH
-        )
-        return carry
-
-    lax.fori_loop(1, n_slab, greet_slab, 0)
-    lax.fori_loop(1, n_cross, greet_cross, 0)
-
     loads = [
         pltpu.make_async_copy(source, target, load_sem.at[k])
         for k, (source, target) in enumerate(
@@ -151,6 +134,24 @@
     ]
     for k in (0, 1, 2, 6):
         loads[k].start()
+
+    barrier = pltpu.get_barrier_semaphore()
+
+    def greet_slab(off, carry):
+        pl.semaphore_signal(
+            barrier, inc=1, device_id=(lax.rem(s + off, n_slab), c), device_id_type=MESH
+        )
+        return carry
+
+    def greet_cross(off, carry):
+        pl.semaphore_signal(
+            barrier, inc=1, device_id=(s, lax.rem(c + off, n_cross)), device_id_type=MESH
+        )
+        return carry
+
+    lax.fori_loop(1, n_slab, greet_slab, 0)
+    lax.fori_loop(1, n_cross, greet_cross, 0)
+
     for k in (0, 1, 2, 6):
         loads[k].wait()
     for k in (3, 4, 5, 7, 8, 9, 10):
@@ -280,16 +281,26 @@
         rows = slice(64 * m, 64 * m + 64)
         op_stack[rows, :] = stack_columns(blocks_f32[rows, :])
     restrict = restrict_ref[...]
+    scaled_restrict = jnp.dot(
+        coarse_ref[...], restrict, precision=HIGHEST, preferred_element_type=F32
+    )
     short = lax.dot_general(
         blocks_f32[...], restrict, NT, precision=HIGHEST, preferred_element_type=F32
     )
     prolong_stack[...] = stack_columns(short)
     tiny = [
-        jnp.dot(restrict, short[64 * m : 64 * m + 64], precision=HIGHEST, preferred_element_type=F32)
+        jnp.dot(
+            scaled_restrict,
+            short[64 * m : 64 * m + 64],
+            precision=HIGHEST,
+            preferred_element_type=F32,
+        )
         for m in range(13)
     ]
     coarse_stack[...] = stack_columns(jnp.concatenate(tiny + [jnp.zeros((8, 8), F32)], axis=0))
-    restrict_cols = stack_columns(jnp.concatenate([restrict, jnp.zeros_like(restrict)], axis=0))
+    restrict_cols = stack_columns(
+        jnp.concatenate([scaled_restrict, jnp.zeros_like(restrict)], axis=0)
+    )
 
     hot_rows = lax.broadcasted_iota(jnp.int32, (owners, LANES), 0)
     before = jnp.concatenate(
@@ -344,7 +355,10 @@
                 ).start()
                 return carry
 
-            lax.fori_loop(0 if hops(step) else 1, n_cross, one, 0, unroll=True)
+            offsets = sorted(range(n_cross), key=lambda off: abs(2 * off - n_cross))
+            for off in offsets:
+                if off or hops(step):
+                    one(off, 0)
         sent.append(functools.partial(release, turn))
         mail[turn, 1, me] = mail[turn, 0, me]
 
@@ -404,7 +418,9 @@
         collect(turn)
         high, low = parts(read_mail(turn))
         spread = jnp.concatenate([high, low], axis=1).astype(BF16)
-        for pair in range(WIDE * WIDE // 2):
+        copies = halo_copies(coarse_field.at[target], halo_coarse.at[target + 1], target + 2)
+        sent.extend(copy.wait_send for copy in copies)
+        for pair in (0, 1, 6, 7, 2, 3, 4, 5):
             both = dot(spread, owner_hot[:, pair * 2 * LANES : (pair + 1) * 2 * LANES])
             for i in range(2):
                 x, y = (2 * pair + i) // WIDE, (2 * pair + i) % WIDE
@@ -417,6 +433,10 @@
                         value,
                     )
                 coarse_field[target, x, y] = value
+            if pair in (1, 7):
+                copies[pair // 7].start()
+        copies[2].start()
+        copies[3].start()
 
     def own_products(load, stack, rows, extra=None):
         def one(x, carry):
@@ -569,10 +589,7 @@
         second_residue(x, 0)
 
     def coarse_step(value):
-        product = jnp.dot(
-            coarse_ref[...], value, precision=HIGHEST, preferred_element_type=F32
-        )
-        return coarse_keep[0] * product
+        return coarse_keep[0] * value
 
     to_owner_start(1, lambda x, y: coarse_field[2, x, y])
     arrived = to_owner_end(0)
@@ -588,7 +605,6 @@
     first = coarse_step(coarse_res)
     from_owner_start(3, first)
     from_owner_end(3, 0)
-    send_halo(coarse_field.at[0], halo_coarse.at[1], 2)
     own_products(fine_stack(coarse_field, 0), coarse_stack, 8)
     await_halo(coarse_field.at[0], halo_coarse.at[1], 2)
     halo_products(fine_stack(halo_coarse, 1), coarse_stack, 8)
@@ -597,7 +613,6 @@
     second = first + coarse_step(again)
     from_owner_start(4, second)
     from_owner_end(4, 1)
-    send_halo(coarse_field.at[1], halo_coarse.at[2], 3)
 
     def add_prolonged(x, y, value):
         fields[3, x, y] = fields[0, x, y] + value

time: 78.1 us -> 77.5 us (level)
  no operation moved by 1% of the time
where the time goes in v6:
time: 77.5 us; the launch traced here: 77.4 us
  Pallas kernels  76.6 us (99%)
  between operations  0.8 us (1%)
    pallas_call x1, Pallas kernels, local(): pl.pallas_call(functools.partial(cycle, n_slab, n_cross, cap), out_shape=...  75.5 us

profile of v6, /device:TPU:0, one launch (start us, length us, event | category | flops | bytes accessed | tf_op | source)
XLA Modules:
  0.0 77.4 jit_solution(4141400292091579980)
XLA Ops:
  0.6 75.5 %shard_map.122 = (f32[1024,128]{1,0:T(8,128)S(1)}, f32[1024,128]{1,0:T(8,128)S(1)}) custom-call(f32[1024,128]{1,0:T(8,128)} %bitcast.9, s32[16,128]{1,0:T(8,128)} %bitcast.15, f32[16]{0:T(128)} %perm_hbm.1, f32[64,64]{1,0:T(8,128)} %vol_hbm.1, f32[384,64]{1,0:T(8,128)} %bitcast.13, f32[192,64]{1,0:T(8,128)} %bitcast.14, f32[1024,64]{1,0:T(8,128)} %bitcast.10, ...), custom_call_target="tpu_custom_call" | custom-call | flops 7298088960 | bytes 4194304 | tf_op jit(solution)/shard_map/pallas_call | solution.py:740
  76.2 1.0 %shard_map.123 = (f32[1024,128]{1,0:T(8,128)}, f32[1024,128]{1,0:T(8,128)}) custom-call(f32[1024,128]{1,0:T(8,128)S(1)} %get-tuple-element.6.sol_in, f32[1024,128]{1,0:T(8,128)S(1)} %get-tuple-element.7.res_in), custom_call_target="tpu_custom_call" | custom-call | tf_op jit(solution)/shard_map/pallas_call | solution.py:751
